TPU v7x, 256 devices: a whole 4x4x8 slice. The times are simulated.
256 devices in a mesh: dp: 64 (over z_lo, y, x, core), tensor: 4 (over z_hi).
Axes of the slice: x: 4, y: 4, z: 8 (z_hi: 4, z_lo: 2; z = z_hi * 2 + z_lo), core: 2. Of those that a mesh axis runs over, the one named last changes fastest.
Arguments:
- queries: bfloat16 [4, 2, 256, 8192], P(None, None, 'dp', 'tensor'), may hold values from -125 to 125
- fresh_kv: bfloat16 [4, 2, 256, 2, 1024], P(None, None, 'dp', None, 'tensor'), may hold values from -4.5 to 4.5
- kv_cache: bfloat16 [2, 256, 512, 2, 1024], P(None, 'dp', None, None, 'tensor'), may hold values from -6 to 6
- cache_len: int32 [256], P('dp'), may hold values from 1 to 512, 81920 in all
- out_proj: bfloat16 [2, 8192, 8192], P(None, 'tensor', 'dp'), may hold values from -0.5 to 0.5
- finished: int32 [256], P('dp'), may hold values 0 or 1
- resp_len: int32 [256], P('dp'), may hold values from 1 to 128, 20480 in all
- start_shard: int32 [256], P('dp'), may hold values from 0 to 3
- resp_act: bfloat16 [256, 128, 8192], P('dp', None, 'tensor'), may hold values from -130 to 130
- reward_gain: bfloat16 [8192], P('tensor'), may hold values from 0.099609375 to 1.8984375
- reward_weight: bfloat16 [8192, 2048], P('tensor', 'dp'), may hold values from -0.0625 to 0.0625
Outputs:
- decoded: bfloat16 [4, 256, 8192], P(None, 'dp')
- scored: bfloat16 [32768, 2048], P('dp', 'tensor')
All inputs are finite; a program needn't handle non-finite values. No bound on the sum of `cache_len` or of `finished` or of `resp_len` on one device may be relied on, other than what follows from the above.
Results may differ from a plain program's by a relative error of at most 0.0057.
Values may be sent and summed in bfloat16 or wider, within the bound.
A program may use at most 128 MiB of HBM per device.

v0:
```python
import math

import jax
import jax.numpy as jnp
from jax import lax
from jax.sharding import PartitionSpec as P

HEAD = 128
SPREAD = 4


epsilon = 1e-05
masked_score = -1e30


def shifted(block, axis, distance):
    devices = range(lax.axis_size(axis))
    route = [((i - distance) % len(devices), i) for i in devices]
    return lax.ppermute(block, axis, route)


def attend(query, cache_keys, cache_vals, valid_cache, fresh_keys, fresh_vals, valid_fresh):
    scale = 1.0 / math.sqrt(query.shape[-1])
    cache_scores = (
        jnp.einsum("rkgd,rpkd->rkgp", query, cache_keys, preferred_element_type=jnp.float32) * scale
    )
    fresh_scores = (
        jnp.einsum("rkgd,rpkd->rkgp", query, fresh_keys, preferred_element_type=jnp.float32) * scale
    )
    cache_scores = jnp.where(valid_cache[:, None, None, :], cache_scores, masked_score)
    fresh_scores = jnp.where(valid_fresh[:, None, None, :], fresh_scores, masked_score)
    peak = jnp.maximum(cache_scores.max(-1), fresh_scores.max(-1))[..., None]
    cache_exp = jnp.exp(cache_scores - peak)
    fresh_exp = jnp.exp(fresh_scores - peak)
    total = cache_exp.sum(-1, keepdims=True) + fresh_exp.sum(-1, keepdims=True)
    cache_w = (cache_exp / total).astype(jnp.bfloat16)
    fresh_w = (fresh_exp / total).astype(jnp.bfloat16)
    result = jnp.einsum("rkgp,rpkd->rkgd", cache_w, cache_vals, preferred_element_type=jnp.float32)
    result = result + jnp.einsum(
        "rkgp,rpkd->rkgd", fresh_w, fresh_vals, preferred_element_type=jnp.float32
    )
    return result.astype(jnp.bfloat16).reshape(query.shape[0], -1)


def project_layer(heads_out, weight):
    return jnp.dot(
        lax.all_gather(heads_out, "dp", axis=0, tiled=True),
        weight,
        preferred_element_type=jnp.float32,
    )


def pick_block(folded, start_shard, offset):
    block = jnp.mod(offset - start_shard, SPREAD)
    return jnp.take_along_axis(folded, block[:, None, None, None], axis=1)[:, 0]


def score(rows, reward_gain, reward_weight):
    floats = rows.astype(jnp.float32)
    squares = lax.psum(jnp.sum(floats * floats, axis=-1), "tensor")
    features = rows.shape[-1] * lax.axis_size("tensor")
    scale = lax.rsqrt(squares / features + epsilon)
    normed = (floats * scale[:, None] * reward_gain.astype(jnp.float32)).astype(jnp.bfloat16)
    partial_cols = jnp.dot(
        normed,
        lax.all_gather(reward_weight, "dp", axis=1, tiled=True),
        preferred_element_type=jnp.float32,
    )
    return lax.psum_scatter(partial_cols, "tensor", scatter_dimension=1, tiled=True).astype(
        jnp.bfloat16
    )


def shards(
    queries,
    fresh_kv,
    kv_cache,
    cache_len,
    out_proj,
    finished,
    resp_len,
    start_shard,
    resp_act,
    reward_gain,
    reward_weight,
):
    rows_here = queries.shape[2]
    step_count = queries.shape[0]
    layer_count = queries.shape[1]
    head_dim = HEAD
    kv_local = kv_cache.shape[-1] // head_dim
    group = queries.shape[-1] // (kv_local * head_dim)
    cache_size = kv_cache.shape[2]
    valid_cache = jnp.arange(cache_size, dtype=jnp.int32)[None, :] < cache_len[:, None]
    outputs = []
    for step_no in range(step_count):
        valid_fresh = jnp.broadcast_to(
            jnp.arange(step_count, dtype=jnp.int32) <= step_no, (rows_here, step_count)
        )
        heads_out = []
        for layer_no in range(layer_count):
            query = queries[step_no, layer_no].reshape(rows_here, kv_local, group, head_dim)
            cache_keys = kv_cache[layer_no, :, :, 0].reshape(
                rows_here, cache_size, kv_local, head_dim
            )
            cache_vals = kv_cache[layer_no, :, :, 1].reshape(
                rows_here, cache_size, kv_local, head_dim
            )
            fresh = jnp.swapaxes(fresh_kv[:, layer_no], 0, 1)
            fresh_keys = fresh[:, :, 0].reshape(rows_here, step_count, kv_local, head_dim)
            fresh_vals = fresh[:, :, 1].reshape(rows_here, step_count, kv_local, head_dim)
            heads_out.append(
                attend(
                    query, cache_keys, cache_vals, valid_cache, fresh_keys, fresh_vals, valid_fresh
                )
            )
        partial_rows = project_layer(heads_out[0], out_proj[0])
        layer_no = 1
        partial_rows = partial_rows + project_layer(heads_out[layer_no], out_proj[layer_no])
        summed = lax.psum(partial_rows, "tensor")
        total = lax.all_to_all(
            summed.astype(jnp.bfloat16), "dp", split_axis=0, concat_axis=1, tiled=True
        ).astype(summed.dtype)
        outputs.append(total.astype(jnp.bfloat16))
    decoded = jnp.stack(outputs)
    resp_count = resp_act.shape[1]
    quart = resp_count // SPREAD
    live = (finished[:, None] == 1) & (
        jnp.arange(resp_count, dtype=jnp.int32)[None, :] < resp_len[:, None]
    )
    masked = resp_act * live[:, :, None].astype(resp_act.dtype)
    folded = masked.reshape(rows_here, SPREAD, quart, masked.shape[-1])
    arrived = []
    for offset in range(SPREAD):
        piece = pick_block(folded, start_shard, offset)
        if offset == 0:
            arrived.append(piece)
        else:
            arrived.append(shifted(piece, "dp", offset))
    gathered = jnp.stack(arrived)
    scored = score(gathered.reshape(-1, gathered.shape[-1]), reward_gain, reward_weight)
    return (decoded, scored)


def solution(mesh):
    return jax.shard_map(
        shards,
        mesh=mesh,
        in_specs=(
            P(None, None, "dp", "tensor"),
            P(None, None, "dp", None, "tensor"),
            P(None, "dp", None, None, "tensor"),
            P("dp"),
            P(None, "tensor", "dp"),
            P("dp"),
            P("dp"),
            P("dp"),
            P("dp", None, "tensor"),
            P("tensor"),
            P("tensor", "dp"),
        ),
        out_specs=(P(None, "dp", None), P("dp", "tensor")),
        check_vma=False,
    )
```

profile of v0, /device:TPU:1, one launch (start us, length us, event | category | flops | bytes accessed | tf_op | source)
XLA Modules:
  0.0 1121.1 jit_solution(9143626471746863446)
XLA Ops:
  7.2 10.8 fusion.172
  18.0 5.8 copy.90
  23.9 4.6 copy.89
  29.5 1.6 fusion.64
  31.3 0.6 reshape.284
  32.0 4.2 copy.92
  36.2 4.6 copy.91
  41.5 1.6 fusion.65
  43.4 0.6 reshape.286
  45.5 0.6 reshape.280
  46.9 1.6 fusion.63
  48.7 0.6 reshape.282
  50.8 0.6 reshape.276
  52.2 1.6 fusion.61
  54.1 0.6 reshape.278
  56.1 0.6 reshape.272
  58.2 0.6 reshape.274
  58.9 0.7 all-gather.18.cloned.1.call-update
  59.8 1.8 broadcast_multiply_fusion
  61.6 0.6 gather_fusion.3
  62.2 0.9 fusion.26
  63.1 4.1 collective-permute-start.2
  67.3 0.6 gather_fusion.2
  67.9 1.0 fusion.27
  69.1 1.5 gather_fusion.1
  70.6 2.0 fusion.28
  72.9 1.4 gather_fusion
  74.3 1.2 fusion.29
  75.4 8.6 collective-permute-done.2
  84.1 11.5 %collective-permute-done.1 = bf16[4,32,2048]{2,1,0:T(8,128)(2,1)S(1)} collective-permute-done((bf16[4,32,2048]{2,1,0:T(8,128)(2,1)}, bf16[4,32,2048]{2,1,0:T(8,128)(2,1)S(1)}, u32[]{:S(2)}, u32[]{:S(2)}) %collective-permute-start.1) | collective-permute-done | bytes 524320 | tf_op jit(solution)/shard_map/ppermute | solution.py:19
  95.6 1.8 collective-permute-done
  97.4 1.5 multiply_reduce_fusion
  99.0 3.4 maximum_convert_fusion
  102.4 65.0 %all-gather.32.cloned.1.call-done = bf16[64,4,2048]{2,1,0:T(4,128)(2,1)} async-done(((bf16[1,4,2048]{2,1,0:T(4,128)(2,1)}), bf16[64,4,2048]{2,1,0:T(4,128)(2,1)}) %all-gather.32.cloned.1.call-update) | async-done | bytes 1048592 | tf_op jit(solution)/shard_map/all_gather | solution.py:47
  167.4 1.3 reshape.285
  168.7 102.0 %all-gather.34.cloned.1.call-done = bf16[64,4,2048]{2,1,0:T(4,128)(2,1)} async-done(((bf16[1,4,2048]{2,1,0:T(4,128)(2,1)}), bf16[64,4,2048]{2,1,0:T(4,128)(2,1)}) %all-gather.34.cloned.1.call-update) | async-done | bytes 1048592 | tf_op jit(solution)/shard_map/all_gather | solution.py:47
  270.7 1.3 reshape.287
  272.0 0.4 fusion.34
  272.9 102.3 %all-gather.28.cloned.1.call-done = bf16[64,4,2048]{2,1,0:T(4,128)(2,1)} async-done(((bf16[1,4,2048]{2,1,0:T(4,128)(2,1)}), bf16[64,4,2048]{2,1,0:T(4,128)(2,1)}) %all-gather.28.cloned.1.call-update) | async-done | bytes 1048592 | tf_op jit(solution)/shard_map/all_gather | solution.py:47
  375.2 1.3 reshape.281
  376.6 103.0 %all-gather.30.cloned.1.call-done = bf16[64,4,2048]{2,1,0:T(4,128)(2,1)} async-done(((bf16[1,4,2048]{2,1,0:T(4,128)(2,1)}), bf16[64,4,2048]{2,1,0:T(4,128)(2,1)}) %all-gather.30.cloned.1.call-update) | async-done | bytes 1048592 | tf_op jit(solution)/shard_map/all_gather | solution.py:47
  479.6 1.3 reshape.283
  480.9 0.4 fusion.36
  481.8 102.2 %all-gather.24.cloned.1.call-done = bf16[64,4,2048]{2,1,0:T(4,128)(2,1)} async-done(((bf16[1,4,2048]{2,1,0:T(4,128)(2,1)}), bf16[64,4,2048]{2,1,0:T(4,128)(2,1)}) %all-gather.24.cloned.1.call-update) | async-done | bytes 1048592 | tf_op jit(solution)/shard_map/all_gather | solution.py:47
  584.0 1.3 reshape.277
  585.3 103.0 %all-gather.26.cloned.1.call-done = bf16[64,4,2048]{2,1,0:T(4,128)(2,1)} async-done(((bf16[1,4,2048]{2,1,0:T(4,128)(2,1)}), bf16[64,4,2048]{2,1,0:T(4,128)(2,1)}) %all-gather.26.cloned.1.call-update) | async-done | bytes 1048592 | tf_op jit(solution)/shard_map/all_gather | solution.py:47
  688.4 1.3 reshape.279
  689.7 0.4 fusion.38
  690.6 102.3 %all-gather.20.cloned.1.call-done = bf16[64,4,2048]{2,1,0:T(4,128)(2,1)} async-done(((bf16[1,4,2048]{2,1,0:T(4,128)(2,1)}), bf16[64,4,2048]{2,1,0:T(4,128)(2,1)}) %all-gather.20.cloned.1.call-update) | async-done | bytes 1048592 | tf_op jit(solution)/shard_map/all_gather | solution.py:47
  792.9 1.3 reshape.273
  794.2 103.2 %all-gather.22.cloned.1.call-done = bf16[64,4,2048]{2,1,0:T(4,128)(2,1)} async-done(((bf16[1,4,2048]{2,1,0:T(4,128)(2,1)}), bf16[64,4,2048]{2,1,0:T(4,128)(2,1)}) %all-gather.22.cloned.1.call-update) | async-done | bytes 1048592 | tf_op jit(solution)/shard_map/all_gather | solution.py:47
  897.4 1.3 reshape.275
  898.8 0.4 fusion.40
  899.6 37.5 %all-reduce.2 = (bf16[256,128]{1,0:T(8,128)(2,1)S(1)}, bf16[256,128]{1,0:T(8,128)(2,1)S(1)}, bf16[256,128]{1,0:T(8,128)(2,1)S(1)}, bf16[256,128]{1,0:T(8,128)(2,1)S(1)}, f32[512]{0:T(512)S(1)}) all-reduce(f32[256,128]{1,0:T(8,128)S(1)} %convolution_add_fusion, ...), channel_id=1, replica_groups=mesh['dp'=64,'tensor'=4] {'tensor'}, use_global_device_ids=true, to_apply=%region_35.36 | all-reduce | flops 131584 | bytes 790528 | tf_op jit(solution)/shard_map/psum | solution.py:120
  937.1 2.6 fusion.1
  939.8 77.5 %all-gather.18.cloned.1.call-done = bf16[2048,2048]{0,1:T(8,128)(2,1)} async-done(((bf16[2048,32]{0,1:T(8,128)(2,1)}), bf16[2048,2048]{0,1:T(8,128)(2,1)}) %all-gather.18.cloned.1.call-update) | async-done | bytes 8388624 | tf_op jit(solution)/shard_map/all_gather | solution.py:66
  1017.2 9.4 fusion.191
  1026.7 15.5 %all_to_all.64 = bf16[64,4,128]{2,1,0:T(4,128)(2,1)S(1)} all-to-all(bf16[64,4,128]{2,1,0:T(4,128)(2,1)S(1)} %bitcast.373), channel_id=1, replica_groups=mesh['dp'=64,'tensor'=4] {'dp'}, dimensions={0} | all-to-all | bytes 131072 | tf_op jit(solution)/shard_map/all_to_all | solution.py:121
  1042.2 14.9 %all_to_all.65 = bf16[64,4,128]{2,1,0:T(4,128)(2,1)S(1)} all-to-all(bf16[64,4,128]{2,1,0:T(4,128)(2,1)S(1)} %bitcast.372), channel_id=1, replica_groups=mesh['dp'=64,'tensor'=4] {'dp'}, dimensions={0} | all-to-all | bytes 131072 | tf_op jit(solution)/shard_map/all_to_all | solution.py:121
  1057.1 14.8 %all_to_all.66 = bf16[64,4,128]{2,1,0:T(4,128)(2,1)S(1)} all-to-all(bf16[64,4,128]{2,1,0:T(4,128)(2,1)S(1)} %bitcast.371), channel_id=1, replica_groups=mesh['dp'=64,'tensor'=4] {'dp'}, dimensions={0} | all-to-all | bytes 131072 | tf_op jit(solution)/shard_map/all_to_all | solution.py:121
  1071.9 13.0 %all_to_all.67 = bf16[64,4,128]{2,1,0:T(4,128)(2,1)S(1)} all-to-all(bf16[64,4,128]{2,1,0:T(4,128)(2,1)S(1)} %bitcast.370), channel_id=1, replica_groups=mesh['dp'=64,'tensor'=4] {'dp'}, dimensions={0} | all-to-all | bytes 131072 | tf_op jit(solution)/shard_map/all_to_all | solution.py:121
  1084.9 0.9 pad_maximum_fusion
  1085.8 26.3 %reduce-scatter.2.cloned.1.call-done = f32[512,512]{1,0:T(8,128)} async-done(((f32[512,2048]{1,0:T(8,128)}), f32[512,512]{1,0:T(8,128)}) %reduce-scatter.2.cloned.1.call-update) | async-done | bytes 1048592 | tf_op jit(solution)/shard_map/reduce_scatter | solution.py:69
  1112.2 2.1 convert_element_type.152
  (128 shorter events, 12.4 us)
Async XLA Ops:
  7.2 160.2 %all-gather.32.cloned.1.call-start = ((), (), s32[]{:S(2)}) async-start(), calls=%async_computation.13 | async-start | bytes 1064960 | tf_op jit(solution)/shard_map/all_gather | solution.py:47
  23.9 4.6 copy-start.3
  23.9 4.7 copy-start.7
  23.9 4.8 copy-start.4
  32.0 238.7 %all-gather.34.cloned.1.call-start = ((), (), s32[]{:S(2)}) async-start(), calls=%async_computation.14 | async-start | bytes 1064960 | tf_op jit(solution)/shard_map/all_gather | solution.py:47
  41.0 3.9 copy-start.1
  44.0 331.2 %all-gather.28.cloned.1.call-start = ((), (), s32[]{:S(2)}) async-start(), calls=%async_computation.11 | async-start | bytes 1064960 | tf_op jit(solution)/shard_map/all_gather | solution.py:47
  46.1 433.5 %all-gather.30.cloned.1.call-start = ((), (), s32[]{:S(2)}) async-start(), calls=%async_computation.12 | async-start | bytes 1064960 | tf_op jit(solution)/shard_map/all_gather | solution.py:47
  49.4 534.6 %all-gather.24.cloned.1.call-start = ((), (), s32[]{:S(2)}) async-start(), calls=%async_computation.9 | async-start | bytes 1064960 | tf_op jit(solution)/shard_map/all_gather | solution.py:47
  51.4 636.9 %all-gather.26.cloned.1.call-start = ((), (), s32[]{:S(2)}) async-start(), calls=%async_computation.10 | async-start | bytes 1064960 | tf_op jit(solution)/shard_map/all_gather | solution.py:47
  54.7 738.2 %all-gather.20.cloned.1.call-start = ((), (), s32[]{:S(2)}) async-start(), calls=%async_computation.7 | async-start | bytes 1064960 | tf_op jit(solution)/shard_map/all_gather | solution.py:47
  55.2 2.3 copy-start.2
  55.5 4.1 copy-start.6
  55.5 4.2 copy-start.9
  55.5 4.2 copy-start.8
  56.8 840.6 %all-gather.22.cloned.1.call-start = ((), (), s32[]{:S(2)}) async-start(), calls=%async_computation.8 | async-start | bytes 1064960 | tf_op jit(solution)/shard_map/all_gather | solution.py:47
  58.8 958.4 %all-gather.18.cloned.1.call-start = ((), (), s32[]{:S(2)}) async-start(), calls=%async_computation.5 | async-start | bytes 8519680 | tf_op jit(solution)/shard_map/all_gather | solution.py:66
  59.6 1052.6 %reduce-scatter.2.cloned.1.call-start = ((), (), s32[]{:S(2)}) async-start(), calls=%async_computation.6 | async-start | bytes 5242880 | tf_op jit(solution)/shard_map/reduce_scatter | solution.py:69
  63.1 21.0 %collective-permute-start.2 = (bf16[4,32,2048]{2,1,0:T(8,128)(2,1)}, bf16[4,32,2048]{2,1,0:T(8,128)(2,1)S(1)}, u32[]{:S(2)}, u32[]{:S(2)}) collective-permute-start(bf16[4,32,2048]{2,1,0:T(8,128)(2,1)} %fusion.26), channel_id=1, source_target_pairs={{244,0},{248,4},{252,8},{0,12},{4,16},{8,20},{12,24},{16,28},{20,3... | collective-permute-start | bytes 1572872 | tf_op jit(solution)/shard_map/ppermute | solution.py:19
  67.8 6.4 copy-start.5
  68.8 26.8 %collective-permute-start.1 = (bf16[4,32,2048]{2,1,0:T(8,128)(2,1)}, bf16[4,32,2048]{2,1,0:T(8,128)(2,1)S(1)}, u32[]{:S(2)}, u32[]{:S(2)}) collective-permute-start(bf16[4,32,2048]{2,1,0:T(8,128)(2,1)} %fusion.27), channel_id=1, source_target_pairs={{248,0},{252,4},{0,8},{4,12},{8,16},{12,20},{16,24},{20,28},{24,32... | collective-permute-start | bytes 1572872 | tf_op jit(solution)/shard_map/ppermute | solution.py:19
  72.6 24.8 %collective-permute-start = (bf16[4,32,2048]{2,1,0:T(8,128)(2,1)}, bf16[4,32,2048]{2,1,0:T(8,128)(2,1)}, u32[]{:S(2)}, u32[]{:S(2)}) collective-permute-start(bf16[4,32,2048]{2,1,0:T(8,128)(2,1)} %fusion.28), channel_id=1, source_target_pairs={{252,0},{0,4},{4,8},{8,12},{12,16},{16,20},{20,24},{24,28},{28,32}... | collective-permute-start | bytes 1572872 | tf_op jit(solution)/shard_map/ppermute | solution.py:19
  102.4 169.6 %copy-start = (bf16[2,2048,128]{2,1,0:T(8,128)(2,1)S(1)}, bf16[2,2048,128]{2,1,0:T(8,128)(2,1)}, u32[]{:S(2)}) copy-start(bf16[2,2048,128]{2,1,0:T(8,128)(2,1)} %param.17) | copy-start | bytes 3145732
Sparse Core Ops, SparseCore 0:
  32.1 135.2 all-gather.31
  169.2 101.4 all-gather.33
  272.6 102.6 all-gather.27
  376.9 102.6 all-gather.29
  481.3 102.6 all-gather.23
  585.7 102.6 all-gather.25
  690.2 102.6 all-gather.19
  794.7 102.6 all-gather.21
  899.3 117.9 all-gather.17
  1026.8 85.3 reduce-scatter.1
where the time goes:
time: 1120 us
  waiting for transfers between devices  910 us (81%)
  blocking collectives  95.7 us (9%)
  local copies, waits for them, and re-layouts  49.9 us (4%)
  matrix products  26.6 us (2%)
  other arithmetic  19.5 us (2%)
  between operations  14.7 us (1%)
    all_gather x8, waiting for transfers between devices, project_layer(): lax.all_gather(heads_out, 'dp', axis=0, tiled=True)  783 us
    all_gather x1, waiting for transfers between devices, score(): lax.all_gather(reward_weight, 'dp', axis=1, tiled=True)  77.5 us
    all_to_all x4, blocking collectives, shards(): lax.all_to_all(summed.astype(jnp.bfloat16), 'dp', split_axis=0, concat_ax...  58.2 us
    psum x1, blocking collectives, shards(): summed = lax.psum(partial_rows, 'tensor')  37.5 us
    unnamed x41, local copies, waits for them, and re-layouts  34.9 us
    reduce_scatter x1, waiting for transfers between devices, score(): lax.psum_scatter(partial_cols, 'tensor', scatter_dimension=1, tiled=True)  26.3 us
  transfers between devices with their start and end apart: 13, of which 13 were waited for; matrix products, arithmetic and copies ran while one was open for 5% of the time, Pallas kernels for 0%

commit v1 on v0

v1 whole, which is shorter than its diff:
```python
import math

import jax
import jax.numpy as jnp
from jax import lax
from jax.sharding import PartitionSpec as P

HEAD = 128
SPREAD = 4


epsilon = 1e-05
masked_score = -1e30


def shifted(block, axis, distance):
    devices = range(lax.axis_size(axis))
    route = [((i - distance) % len(devices), i) for i in devices]
    return lax.ppermute(block, axis, route)


def attend(queries, fresh_kv, kv_cache, cache_len):
    steps, layers, rows, width = queries.shape
    cache = kv_cache.shape[2]
    kvs = kv_cache.shape[-1] // HEAD
    group = width // (kvs * HEAD)
    scale = 1.0 / math.sqrt(HEAD)
    q = queries.reshape(steps, layers, rows, kvs, group, HEAD)
    c = kv_cache.reshape(layers, rows, cache, 2, kvs, HEAD)
    f = fresh_kv.reshape(steps, layers, rows, 2, kvs, HEAD)
    cs = jnp.einsum("slrkgd,lrpkd->lrksgp", q, c[:, :, :, 0], preferred_element_type=jnp.float32) * scale
    fs = jnp.einsum("slrkgd,ulrkd->lrksgu", q, f[:, :, :, 0], preferred_element_type=jnp.float32) * scale
    valid = jnp.arange(cache, dtype=jnp.int32)[None, :] < cache_len[:, None]
    cs = jnp.where(valid[None, :, None, None, None, :], cs, masked_score)
    order = jnp.arange(steps, dtype=jnp.int32)
    seen = order[None, :] <= order[:, None]
    fs = jnp.where(seen[None, None, None, :, None, :], fs, masked_score)
    peak = jnp.maximum(cs.max(-1), fs.max(-1))[..., None]
    ce = jnp.exp(cs - peak)
    fe = jnp.exp(fs - peak)
    total = ce.sum(-1, keepdims=True) + fe.sum(-1, keepdims=True)
    cw = (ce / total).astype(jnp.bfloat16)
    fw = (fe / total).astype(jnp.bfloat16)
    out = jnp.einsum("lrksgp,lrpkd->rslkgd", cw, c[:, :, :, 1], preferred_element_type=jnp.float32)
    out = out + jnp.einsum("lrksgu,ulrkd->rslkgd", fw, f[:, :, :, 1], preferred_element_type=jnp.float32)
    return out.astype(jnp.bfloat16).reshape(rows * steps, layers * width)


def shards(
    queries,
    fresh_kv,
    kv_cache,
    cache_len,
    out_proj,
    finished,
    resp_len,
    start_shard,
    resp_act,
    reward_gain,
    reward_weight,
):
    steps, layers, rows, width = queries.shape
    groups = lax.axis_size("dp")
    heads = attend(queries, fresh_kv, kv_cache, cache_len)
    weight = lax.all_gather(reward_weight, "dp", axis=1, tiled=True)
    heads = lax.all_gather(heads, "dp", axis=0, tiled=True)
    part = jnp.dot(heads, out_proj.reshape(layers * width, -1), preferred_element_type=jnp.float32)
    summed = lax.psum(part, "tensor").astype(jnp.bfloat16)
    moved = lax.all_to_all(
        summed.reshape(groups, rows, steps, -1), "dp", split_axis=0, concat_axis=0, tiled=True
    )
    decoded = moved.transpose(2, 1, 0, 3).reshape(steps, rows, -1)

    count = resp_act.shape[1]
    quart = count // SPREAD
    live = (finished[:, None] == 1) & (
        jnp.arange(count, dtype=jnp.int32)[None, :] < resp_len[:, None]
    )
    masked = resp_act * live[:, :, None].astype(resp_act.dtype)
    folded = masked.reshape(rows, SPREAD, quart, -1)
    offset = jnp.arange(SPREAD, dtype=jnp.int32)
    block = jnp.mod(offset[None, :] - start_shard[:, None], SPREAD)
    turned = jnp.take_along_axis(folded, block[:, :, None, None], axis=1)
    turned = turned.transpose(1, 0, 2, 3).reshape(SPREAD * rows * quart, -1)
    floats = turned.astype(jnp.float32)
    squares = lax.psum(jnp.sum(floats * floats, axis=-1), "tensor")
    features = turned.shape[-1] * lax.axis_size("tensor")
    scale = lax.rsqrt(squares / features + epsilon)
    normed = (floats * scale[:, None] * reward_gain.astype(jnp.float32)).astype(jnp.bfloat16)
    cols = jnp.dot(normed, weight, preferred_element_type=jnp.float32)
    mine = lax.psum_scatter(cols, "tensor", scatter_dimension=1, tiled=True).astype(jnp.bfloat16)
    mine = mine.reshape(SPREAD, rows * quart, -1)
    scored = jnp.concatenate([mine[0]] + [shifted(mine[k], "dp", k) for k in range(1, SPREAD)])
    return (decoded, scored)


def solution(mesh):
    return jax.shard_map(
        shards,
        mesh=mesh,
        in_specs=(
            P(None, None, "dp", "tensor"),
            P(None, None, "dp", None, "tensor"),
            P(None, "dp", None, None, "tensor"),
            P("dp"),
            P(None, "tensor", "dp"),
            P("dp"),
            P("dp"),
            P("dp"),
            P("dp", None, "tensor"),
            P("tensor"),
            P("tensor", "dp"),
        ),
        out_specs=(P(None, "dp", None), P("dp", "tensor")),
        check_vma=False,
    )
```

time: 1120 us -> 385 us (0.34)
  waiting for transfers between devices: 910 us -> 265 us
  blocking collectives: 95.7 us -> 37.9 us
  local copies, waits for them, and re-layouts: 49.9 us -> 24.7 us
  other arithmetic: 19.5 us -> 8.22 us
    all_gather x9 -> x2, waiting for transfers between devices: 860 us -> 185 us  [the longest x1 110 us: shards(): heads = lax.all_gather(heads, 'dp', axis=0, tiled=True)]
    all_to_all x4 -> x0, blocking collectives: 58.2 us -> none  [shards(): lax.all_to_all(summed.astype(jnp.bfloat16), 'dp', split_axis=0, concat_ax...]
    reduce_scatter x1, waiting for transfers between devices: 26.3 us -> 70.4 us  [shards(): lax.psum_scatter(cols, 'tensor', scatter_dimension=1, tiled=True)]
    unnamed x41 -> x20, local copies, waits for them, and re-layouts: 34.9 us -> 14.6 us
    ppermute x3, waiting for transfers between devices: 22 us -> 9.09 us  [shifted(): return lax.ppermute(block, axis, route)]
    dot_general x41 -> x6, matrix products: 26.6 us -> 19.2 us  [the longest x1 9.45 us: shards(): cols = jnp.dot(normed, weight, preferred_element_type=jnp.float32)]
  transfers between devices with their start and end apart: 13 -> 7, of which waited for: 13 -> 5; matrix products, arithmetic and copies ran while one was open for 5% -> 5% of each run, Pallas kernels for 0% -> 0%
where the time goes in v1:
time: 385 us; the launch traced here: 384 us
  waiting for transfers between devices  265 us (69%)
  blocking collectives  37.9 us (10%)
  local copies, waits for them, and re-layouts  24.7 us (6%)
  matrix products  19.2 us (5%)
  starting transfers between devices  14.4 us (4%)
  between operations  13.9 us (4%)
  other arithmetic  8.22 us (2%)
    all_gather x1, waiting for transfers between devices, shards(): heads = lax.all_gather(heads, 'dp', axis=0, tiled=True)  110 us
    all_gather x1, waiting for transfers between devices, shards(): weight = lax.all_gather(reward_weight, 'dp', axis=1, tiled=True)  75.3 us
    reduce_scatter x1, waiting for transfers between devices, shards(): lax.psum_scatter(cols, 'tensor', scatter_dimension=1, tiled=True)  70.4 us
    psum x1, blocking collectives, shards(): summed = lax.psum(part, 'tensor').astype(jnp.bfloat16)  37.9 us
    unnamed x20, local copies, waits for them, and re-layouts  14.6 us
    dot_general x1, matrix products, shards(): cols = jnp.dot(normed, weight, preferred_element_type=jnp.float32)  9.45 us
    ppermute x3, waiting for transfers between devices, shifted(): return lax.ppermute(block, axis, route)  9.09 us
  transfers between devices with their start and end apart: 7, of which 5 were waited for; matrix products, arithmetic and copies ran while one was open for 5% of the time, Pallas kernels for 0%

profile of v1, /device:TPU:1, one launch (start us, length us, event | category | flops | bytes accessed | tf_op | source)
XLA Modules:
  0.0 383.5 jit_solution(8334101828547246645)
XLA Ops:
  7.2 0.0 copy-start
  7.2 0.0 all-gather.3.cloned.1.call-start
  7.2 0.9 reshape.226
  8.1 1.0 reshape.224
  9.1 0.0 copy-start.5
  9.1 11.1 %copy.55 = bf16[2,4,512,2,256]{2,4,3,1,0:T(8,128)(2,1)} copy(bf16[2,4,512,2,256]{4,3,2,1,0:T(2,128)(2,1)} %param.13) | data formatting | bytes 8388608 | tf_op args[2]
  20.3 0.0 copy-done.5
  20.3 0.1 iota_compare_fusion
  20.3 0.0 copy-start.1
  20.3 1.9 slice.40
  22.3 0.9 copy-done.1
  23.1 0.5 fusion.33
  23.7 0.7 fusion.34
  24.4 0.3 copy-done.2
  24.7 0.3 fusion.17
  25.0 0.1 fusion.21
  25.1 2.4 copy.74
  27.5 0.3 fusion.22
  27.8 0.0 copy-start.8
  27.8 0.0 copy-start.7
  27.8 0.0 copy-start.3
  27.8 2.6 fusion.13
  30.4 0.7 reshape.227
  31.1 0.0 all-gather.3.cloned.1.call-update
  31.2 0.0 all-gather.5.cloned.1.call-start
  31.2 0.7 all-gather.5.cloned.1.call-update
  31.9 0.0 reduce-scatter.2.cloned.1.call-start
  32.0 0.0 copy-done.6
  32.0 0.1 fusion.28
  32.1 0.1 reshape.233
  32.1 0.0 copy-done.8
  32.1 0.0 copy-done.7
  32.2 0.1 fusion.30
  32.2 0.0 copy-done.3
  32.2 1.6 broadcast_multiply_fusion
  33.8 2.3 gather_fusion
  36.1 0.1 compare_and_fusion
  36.2 0.7 multiply_reduce_fusion
  36.9 0.1 reduce_sum.32
  37.0 0.3 select_convert_fusion
  37.3 0.0 copy-start.4
  37.3 2.2 copy.66
  39.5 0.0 copy-done.4
  39.5 109.6 %all-gather.3.cloned.1.call-done = bf16[1024,4096]{1,0:T(8,128)(2,1)} async-done(((bf16[16,4096]{1,0:T(8,128)(2,1)}), bf16[1024,4096]{1,0:T(8,128)(2,1)}) %all-gather.3.cloned.1.call-update) | async-done | bytes 8388624 | tf_op jit(solution)/shard_map/all_gather | solution.py:66
  149.1 0.0 copy-done
  149.1 5.7 %fusion.35 = f32[1024,128]{1,0:T(8,128)S(1)} fusion(bf16[1024,4096]{1,0:T(8,128)(2,1)} %all-gather.3.cloned.1.call-done, bf16[4096,128]{1,0:T(8,128)(2,1)S(1)} %bitcast.66), kind=kOutput, calls=%fused_computation.57 | convolution fusion | flops 1073741824 | bytes 9961472 | tf_op jit(solution)/shard_map/dot_general | solution.py:67
  154.8 37.9 %all-reduce.2 = (bf16[1024,128]{1,0:T(8,128)(2,1)}, f32[512]{0:T(512)S(1)}) all-reduce(f32[1024,128]{1,0:T(8,128)S(1)} %fusion.35, f32[512]{0:T(512)S(1)} %reduce_sum.32), channel_id=1, replica_groups=mesh['dp'=64,'tensor'=4] {'tensor'}, use_global_device_ids=true, to_apply=%region_4.5 | all-reduce | flops 131584 | bytes 790528 | tf_op jit(solution)/shard_map/psum | solution.py:68
  192.7 2.7 fusion.1
  195.4 75.3 %all-gather.5.cloned.1.call-done = bf16[2048,2048]{0,1:T(8,128)(2,1)} async-done(((bf16[2048,32]{0,1:T(8,128)(2,1)}), bf16[2048,2048]{0,1:T(8,128)(2,1)}) %all-gather.5.cloned.1.call-update) | async-done | bytes 8388624 | tf_op jit(solution)/shard_map/all_gather | solution.py:65
  270.7 9.4 %fusion.36 = f32[512,2048]{1,0:T(8,128)} fusion(bf16[512,2048]{1,0:T(8,128)(2,1)S(1)} %fusion.1, bf16[2048,2048]{0,1:T(8,128)(2,1)} %all-gather.5.cloned.1.call-done), kind=kOutput, calls=%fused_computation.58 | convolution fusion | flops 4294967296 | bytes 14680064 | tf_op jit(solution)/shard_map/dot_general | solution.py:90
  280.1 0.0 reduce-scatter.2.cloned.1.call-update
  280.1 7.3 %all-to-all-start = ((bf16[64,4,4,128]{3,2,1,0:T(4,128)(2,1)}), bf16[64,4,4,128]{3,2,1,0:T(4,128)(2,1)S(1)}, u32[]{:S(2)}, u32[]{:S(2)}) async-start(bf16[64,4,4,128]{3,2,1,0:T(4,128)(2,1)} %bitcast.15), calls=%async_computation | async-start | bytes 524288 | tf_op jit(solution)/shard_map/all_to_all | solution.py:69
  287.5 70.4 %reduce-scatter.2.cloned.1.call-done = f32[512,512]{1,0:T(8,128)} async-done(((f32[512,2048]{1,0:T(8,128)}), f32[512,512]{1,0:T(8,128)}) %reduce-scatter.2.cloned.1.call-update) | async-done | bytes 1048592 | tf_op jit(solution)/shard_map/reduce_scatter | solution.py:91
  357.9 1.3 convert_element_type.52
  359.2 6.8 %collective-permute-start.2 = (bf16[128,512]{1,0:T(8,128)(2,1)S(1)}, bf16[128,512]{1,0:T(8,128)(2,1)S(1)}, u32[]{:S(2)}, u32[]{:S(2)}) collective-permute-start(bf16[128,512]{1,0:T(8,128)(2,1)S(1)} %get-tuple-element.5), channel_id=1, source_target_pairs={{244,0},{248,4},{252,8},{0,12},{4,16},{8,20},{12,24},{16,28},{20,3... | collective-permute-start | bytes 393224 | tf_op jit(solution)/shard_map/ppermute | solution.py:19
  366.0 0.2 collective-permute-start.1
  366.2 0.0 collective-permute-start
  366.2 0.0 all-to-all-done
  366.2 0.1 copy.65
  366.3 0.8 reshape.230
  367.1 7.6 %collective-permute-done.2 = bf16[128,512]{1,0:T(8,128)(2,1)S(1)} collective-permute-done((bf16[128,512]{1,0:T(8,128)(2,1)S(1)}, bf16[128,512]{1,0:T(8,128)(2,1)S(1)}, u32[]{:S(2)}, u32[]{:S(2)}) %collective-permute-start.2) | collective-permute-done | bytes 131104 | tf_op jit(solution)/shard_map/ppermute | solution.py:19
  374.7 1.5 collective-permute-done.1
  376.1 0.0 collective-permute-done
  376.1 0.8 pad_maximum_fusion
  (12 shorter events, 0.1 us)
Async XLA Ops:
  7.2 142.0 %copy-start = (bf16[2,2048,128]{2,1,0:T(8,128)(2,1)S(1)}, bf16[2,2048,128]{2,1,0:T(8,128)(2,1)}, u32[]{:S(2)}) copy-start(bf16[2,2048,128]{2,1,0:T(8,128)(2,1)} %param.15) | copy-start | bytes 3145732
  7.2 141.9 %all-gather.3.cloned.1.call-start = ((), (), s32[]{:S(2)}) async-start(), calls=%async_computation.2 | async-start | bytes 8519680 | tf_op jit(solution)/shard_map/all_gather | solution.py:66
  9.1 11.1 %copy-start.5 = (s32[4]{0:T(128)S(1)}, s32[4]{0:T(128)}, u32[]{:S(2)}) copy-start(s32[4]{0:T(128)} %param.14) | copy-start | bytes 52
  20.3 2.8 copy-start.1
  23.7 1.0 copy-start.2
  27.8 4.2 %copy-start.6 = (s32[4]{0:T(128)S(1)}, s32[4]{0:T(128)}, u32[]{:S(2)}) copy-start(s32[4]{0:T(128)} %param.18) | copy-start | bytes 52
  27.8 4.4 %copy-start.8 = (s32[4]{0:T(128)S(1)}, s32[4]{0:T(128)}, u32[]{:S(2)}) copy-start(s32[4]{0:T(128)} %param.16) | copy-start | bytes 52
  27.8 4.4 %copy-start.7 = (s32[4]{0:T(128)S(1)}, s32[4]{0:T(128)}, u32[]{:S(2)}) copy-start(s32[4]{0:T(128)} %param.17) | copy-start | bytes 52
  27.8 4.4 %copy-start.3 = (bf16[4,128,2048]{2,1,0:T(8,128)(2,1)S(1)}, bf16[4,128,2048]{2,1,0:T(8,128)(2,1)}, u32[]{:S(2)}) copy-start(bf16[4,128,2048]{2,1,0:T(8,128)(2,1)} %param.19) | copy-start | bytes 6291460
  31.2 239.5 %all-gather.5.cloned.1.call-start = ((), (), s32[]{:S(2)}) async-start(), calls=%async_computation.3 | async-start | bytes 8519680 | tf_op jit(solution)/shard_map/all_gather | solution.py:65
  31.9 325.9 %reduce-scatter.2.cloned.1.call-start = ((), (), s32[]{:S(2)}) async-start(), calls=%async_computation.4 | async-start | bytes 5242880 | tf_op jit(solution)/shard_map/reduce_scatter | solution.py:91
  37.3 2.2 copy-start.4
  280.1 86.1 %all-to-all-start = ((bf16[64,4,4,128]{3,2,1,0:T(4,128)(2,1)}), bf16[64,4,4,128]{3,2,1,0:T(4,128)(2,1)S(1)}, u32[]{:S(2)}, u32[]{:S(2)}) async-start(bf16[64,4,4,128]{3,2,1,0:T(4,128)(2,1)} %bitcast.15), calls=%async_computation | async-start | bytes 524288 | tf_op jit(solution)/shard_map/all_to_all | solution.py:69
  359.2 15.5 %collective-permute-start.2 = (bf16[128,512]{1,0:T(8,128)(2,1)S(1)}, bf16[128,512]{1,0:T(8,128)(2,1)S(1)}, u32[]{:S(2)}, u32[]{:S(2)}) collective-permute-start(bf16[128,512]{1,0:T(8,128)(2,1)S(1)} %get-tuple-element.5), channel_id=1, source_target_pairs={{244,0},{248,4},{252,8},{0,12},{4,16},{8,20},{12,24},{16,28},{20,3... | collective-permute-start | bytes 393224 | tf_op jit(solution)/shard_map/ppermute | solution.py:19
  366.0 10.2 %collective-permute-start.1 = (bf16[128,512]{1,0:T(8,128)(2,1)S(1)}, bf16[128,512]{1,0:T(8,128)(2,1)S(1)}, u32[]{:S(2)}, u32[]{:S(2)}) collective-permute-start(bf16[128,512]{1,0:T(8,128)(2,1)S(1)} %get-tuple-element.6), channel_id=1, source_target_pairs={{248,0},{252,4},{0,8},{4,12},{8,16},{12,20},{16,24},{20,28},{24,32... | collective-permute-start | bytes 393224 | tf_op jit(solution)/shard_map/ppermute | solution.py:19
  366.2 9.9 %collective-permute-start = (bf16[128,512]{1,0:T(8,128)(2,1)S(1)}, bf16[128,512]{1,0:T(8,128)(2,1)S(1)}, u32[]{:S(2)}, u32[]{:S(2)}) collective-permute-start(bf16[128,512]{1,0:T(8,128)(2,1)S(1)} %get-tuple-element.7), channel_id=1, source_target_pairs={{252,0},{0,4},{4,8},{8,12},{12,16},{16,20},{20,24},{24,28},{28,32}... | collective-permute-start | bytes 393224 | tf_op jit(solution)/shard_map/ppermute | solution.py:19
Sparse Core Ops, SparseCore 0:
  31.3 117.7 all-gather.2
  151.0 119.6 all-gather.4
  280.3 77.5 reduce-scatter.1

commit v2 on v1

v2 whole, which is shorter than its diff:
```python
import functools
import math

import jax
import jax.numpy as jnp
from jax import lax
from jax.experimental import pallas as pl
from jax.experimental.pallas import tpu as pltpu
from jax.sharding import PartitionSpec as P

HEAD = 128
SPREAD = 4
QUART = 32
ROWS_G = 4
TENSOR = 4

epsilon = 1e-05
masked_score = -1e30

MESH = pl.DeviceIdType.MESH
STEP_OFF = (0, 1, -1, 2)
BACK = {1: 2, -1: 1, 2: 3}
F32 = jnp.float32
BF16 = jnp.bfloat16


def wrap(v, n):
    return lax.rem(v + 2 * n, n)


class Place:
    def __init__(self):
        self.dp = lax.axis_index("dp")
        self.t = lax.axis_index("tensor")
        self.core = lax.rem(self.dp, 2)
        self.x = lax.rem(self.dp // 2, 4)
        self.y = lax.rem(self.dp // 8, 4)
        self.zl = self.dp // 32

    def at(self, zl, y, x, core):
        return (((zl * 4 + y) * 4 + x) * 2 + core, self.t)


class Gather:
    def __init__(self, place, own, out, send, recv, local):
        self.p, self.own, self.out, self.send, self.recv, self.local = place, own, out, send, recv, local

    def ring(self, h):
        return (self.p.y, self.p.x) if h == 0 else (self.p.x, self.p.y)

    def dev(self, h, s, f, zl=None, core=None):
        p = self.p
        zl = p.zl if zl is None else zl
        core = p.core if core is None else core
        return p.at(zl, s, f, core) if h == 0 else p.at(zl, f, s, core)

    def unit(self, h, j, core=None):
        s, f = self.ring(h)
        s = wrap(s + STEP_OFF[j // 4], 4)
        f = wrap(f + STEP_OFF[j % 4], 4)
        return self.out.at[h, s, f, :, self.p.core if core is None else core]

    def copy(self, h, src, dst, send, recv, dev):
        return pltpu.make_async_remote_copy(
            src_ref=src, dst_ref=dst, send_sem=self.send.at[h, send], recv_sem=self.recv.at[h, recv],
            device_id=dev, device_id_type=MESH)

    def z_copy(self, h):
        s, f = self.ring(h)
        return self.copy(h, self.own(h), self.out.at[h, s, f, self.p.zl, self.p.core], 0, 0,
                         self.dev(h, s, f, zl=1 - self.p.zl))

    def own_copy(self, h):
        s, f = self.ring(h)
        return pltpu.make_async_copy(self.own(h), self.out.at[h, s, f, self.p.zl, self.p.core], self.local.at[h])

    def start(self):
        for h in range(2):
            self.z_copy(h).start()
            self.own_copy(h).start()

    def first(self, h, i):
        s, f = self.ring(h)
        u = self.unit(h, 0)
        return self.copy(h, u, u, i, BACK[STEP_OFF[i]], self.dev(h, s, wrap(f + STEP_OFF[i], 4)))

    def second(self, h, i, right):
        s, f = self.ring(h)
        u = self.unit(h, i)
        step = 1 if right else -1
        base = 8 if right else 4
        return self.copy(h, u, u, base + i, base + i, self.dev(h, wrap(s + step, 4), f))

    def onward(self, h, i):
        s, f = self.ring(h)
        u = self.unit(h, (8 if i < 2 else 4) + i)
        return self.copy(h, u, u, 12 + i, 12 + i, self.dev(h, wrap(s + (1 if i < 2 else -1), 4), f))

    def across(self, h, j):
        s, f = self.ring(h)
        u = self.unit(h, j)
        return self.copy(h, u, u, 16 + j, 16 + j, self.dev(h, s, f, core=1 - self.p.core))

    def arrived(self, h, j):
        u = self.unit(h, j)
        self.copy(h, u, u, j, j, self.dev(h, *self.ring(h), core=1 - self.p.core)).wait_recv()

    def after_z(self):
        for h in range(2):
            s, f = self.ring(h)
            u = self.out.at[h, s, f, 1 - self.p.zl, self.p.core]
            self.copy(h, u, u, 0, 0, self.dev(h, s, f, zl=1 - self.p.zl)).wait_recv()
            self.own_copy(h).wait()
            for i in (1, 2, 3):
                self.first(h, i).start()
            for right in (True, False):
                self.second(h, 0, right).start()
            self.across(h, 0).start()

    def after_first(self, i):
        for h in range(2):
            self.arrived(h, i)
            for right in (True, False):
                self.second(h, i, right).start()
            self.across(h, i).start()

    def after_second(self, i):
        for h in range(2):
            for j in ((8 + i, 4 + i) if i < 2 else (4 + i, 8 + i)):
                self.arrived(h, j)
                if j == (8 if i < 2 else 4) + i:
                    self.onward(h, i).start()
                self.across(h, j).start()

    def after_onward(self, i):
        for h in range(2):
            self.arrived(h, 12 + i)
            self.across(h, 12 + i).start()

    def after_across(self):
        for h in range(2):
            for j in range(16):
                u = self.unit(h, j, core=1 - self.p.core)
                self.copy(h, u, u, 16 + j, 16 + j, self.dev(h, *self.ring(h), core=1 - self.p.core)).wait_recv()

    def end(self):
        for h in range(2):
            self.z_copy(h).wait_send()
            for i in (1, 2, 3):
                self.first(h, i).wait_send()
            for i in range(4):
                self.second(h, i, True).wait_send()
                self.second(h, i, False).wait_send()
                self.onward(h, i).wait_send()
            for j in range(16):
                self.across(h, j).wait_send()


def eye_mask():
    return lax.broadcasted_iota(jnp.int32, (128, 128), 0) == lax.broadcasted_iota(jnp.int32, (128, 128), 1)


def dot_nt(a, b):
    return lax.dot_general(a, b, (((1,), (1,)), ((), ())), preferred_element_type=F32)


def kernel(
    pick_ref, heads_ref, outp_ref, resp_ref, gain_ref, wt_ref,
    dec_ref, scored_ref,
    gw, gh, normed, pacc, rs_send, rs_recv, dacc, ds_send, ds_recv, dfin, sq_own, sq_got,
    w_send, w_recv, w_local, h_send, h_recv, h_local,
    rss, rsr, dss, dsr, sqs, sqr, rot_s, rot_r, out_s, out_r,
):
    p = Place()
    dp, t = p.dp, p.t
    groups = 64
    width = wt_ref.shape[1]
    half_w = width // 2
    is_self = lax.div(dp, 16) == t

    barrier = pltpu.get_barrier_semaphore()

    def greet(dev):
        pl.semaphore_signal(barrier, inc=1, device_id=dev, device_id_type=MESH)

    greet(p.at(1 - p.zl, p.y, p.x, p.core))
    greet(p.at(p.zl, p.y, p.x, 1 - p.core))
    for d in (1, 2, 3):
        greet(p.at(p.zl, p.y, wrap(p.x + d, 4), p.core))
        greet(p.at(p.zl, wrap(p.y + d, 4), p.x, p.core))
        greet((dp, wrap(t + d, 4)))
        greet((wrap(dp - d, groups), t))

    def greet_source(d, c):
        src_t = lax.div(dp, 16)

        @pl.when(jnp.logical_not(jnp.logical_and(d == dp, src_t == t)))
        def _():
            greet((d, src_t))

        return c

    lax.fori_loop(0, groups, greet_source, 0)
    pl.semaphore_wait(barrier, 14 + groups - is_self.astype(jnp.int32))

    gath_w = Gather(p, lambda h: wt_ref.at[:, pl.ds(h * half_w, half_w)], gw, w_send, w_recv, w_local)
    gath_h = Gather(p, lambda h: heads_ref.at[:, pl.ds(h * width, width)], gh, h_send, h_recv, h_local)
    gath_w.start()
    gath_h.start()

    eye = eye_mask()

    def turn_rows(r, c):
        col = jnp.zeros((128, 1), F32)
        for part in range(4):
            cols = slice(part * (width // 4), (part + 1) * (width // 4))
            block = jnp.dot(pick_ref[r], resp_ref[r, :, cols], preferred_element_type=F32)
            for k in range(SPREAD):
                normed[pl.ds(pl.multiple_of(k * 128 + r * QUART, QUART), QUART), cols] = block[
                    k * QUART:(k + 1) * QUART].astype(BF16)
            col = col + jnp.sum(block * block, axis=1, keepdims=True)
        sq_own[r] = jnp.broadcast_to(jnp.sum(jnp.where(eye, col, 0.0), axis=0, keepdims=True), (8, 128))
        return c

    lax.fori_loop(0, ROWS_G, turn_rows, 0)

    def sq_copy(d):
        return pltpu.make_async_remote_copy(
            src_ref=sq_own, dst_ref=sq_got.at[3 - d], send_sem=sqs.at[d - 1], recv_sem=sqr.at[3 - d],
            device_id=(dp, wrap(t + d, 4)), device_id_type=MESH)

    for d in (1, 2, 3):
        sq_copy(d).start()

    gath_w.after_z()
    for d in (1, 2, 3):
        sq_copy(d).wait()

    def norm_rows(r, c):
        total = sq_own[r] + sq_got[0, r] + sq_got[1, r] + sq_got[2, r]
        scale = lax.rsqrt(total[0:1] / (width * TENSOR) + epsilon)
        col = jnp.sum(jnp.where(eye, scale, 0.0), axis=1, keepdims=True)
        for k in range(SPREAD):
            rows = pl.ds(pl.multiple_of(k * 128 + r * QUART, QUART), QUART)
            block = normed[rows, :].astype(F32) * col[k * QUART:(k + 1) * QUART] * gain_ref[...].astype(F32)
            normed[rows, :] = block.astype(BF16)
        return c

    lax.fori_loop(0, ROWS_G, norm_rows, 0)

    for i in (1, 2, 3):
        gath_w.after_first(i)
    gath_h.after_z()
    for i in range(4):
        gath_w.after_second(i)
    for i in (1, 2, 3):
        gath_h.after_first(i)
    for i in range(4):
        gath_w.after_onward(i)
    gath_w.after_across()

    def direction(k):
        return 1 if k >= 2 else -1

    def project(owner, row0, rows):
        zl = lax.div(owner, 2)

        def tile(y_lo, c):
            y = lax.rem(owner, 2) * 2 + y_lo
            wa = gw[0, y, :, zl].reshape(256, half_w)
            wb = gw[1, :, y, zl].reshape(256, half_w)
            res = dot_nt(normed[row0:row0 + rows, :half_w], wa)
            res = res + dot_nt(normed[row0:row0 + rows, half_w:], wb)
            pacc[row0:row0 + rows, pl.ds(pl.multiple_of(y_lo * 256, 256), 256)] = res
            return c

        lax.fori_loop(0, 2, tile, 0)

    def rs_copy(k, step):
        return pltpu.make_async_remote_copy(
            src_ref=rs_send.at[k, step], dst_ref=rs_recv.at[k, step], send_sem=rss.at[k, step],
            recv_sem=rsr.at[k, step], device_id=(dp, wrap(t + direction(k), 4)), device_id_type=MESH)

    def rot_copy(k):
        rows = scored_ref.at[pl.ds(k * 128, 128), :]
        return pltpu.make_async_remote_copy(
            src_ref=rs_send.at[k, 3], dst_ref=rows, send_sem=rot_s.at[k], recv_sem=rot_r.at[k],
            device_id=(lax.rem(dp + k, groups), t), device_id_type=MESH)

    def project_step(step):
        if step == 1:
            project(wrap(t + 2, 4), 0, 512)
        elif step == 3:
            project(t, 0, 512)
        else:
            project(wrap(t + 1 + step, 4), 0, 256)
            project(wrap(t - 1 - step, 4), 256, 256)

    def pass_step(step):
        for k in (3, 1, 2, 0):
            rows = slice(k * 128, (k + 1) * 128)
            total = pacc[rows, :]
            if step:
                rs_copy(k, step - 1).wait_recv()
                total = total + rs_recv[k, step - 1].astype(F32)
            if step == 3 and k == 0:
                scored_ref[rows, :] = total.astype(BF16)
                continue
            rs_send[k, step] = total.astype(BF16)
            if step < 3:
                rs_copy(k, step).start()
            else:
                rot_copy(k).start()

    project_step(0)
    pass_step(0)
    for i in range(4):
        gath_h.after_second(i)
    project_step(1)
    pass_step(1)
    for i in range(4):
        gath_h.after_onward(i)
    project_step(2)
    gath_h.after_across()

    def decode_part(owner, y_lo):
        zl = lax.div(owner, 2)
        y = lax.rem(owner, 2) * 2 + y_lo
        ha = gh[0, y, :, zl].reshape(128, width)
        hb = gh[1, :, y, zl].reshape(128, width)
        return (jnp.dot(ha, outp_ref[0], preferred_element_type=F32)
                + jnp.dot(hb, outp_ref[1], preferred_element_type=F32))

    def decode_tiles(i, c):
        dacc[i] = decode_part(lax.div(i, 2), lax.rem(i, 2))
        return c

    lax.fori_loop(0, 8, decode_tiles, 0)

    def ds_copy(y_lo, step):
        return pltpu.make_async_remote_copy(
            src_ref=ds_send.at[y_lo, step], dst_ref=ds_recv.at[y_lo, step], send_sem=dss.at[y_lo, step],
            recv_sem=dsr.at[y_lo, step], device_id=(dp, wrap(t + (1 if y_lo else -1), 4)), device_id_type=MESH)

    def decode_step(step):
        for y_lo in range(2):
            owner = wrap(t - (1 + step) * (1 if y_lo else -1), 4)
            total = dacc[owner * 2 + y_lo]
            if step:
                ds_copy(y_lo, step - 1).wait_recv()
                total = total + ds_recv[y_lo, step - 1].astype(F32)
            if step < 3:
                ds_send[y_lo, step] = total.astype(BF16)
                ds_copy(y_lo, step).start()
            else:
                dfin[pl.ds(y_lo * 8, 8)] = total.astype(BF16).reshape(8, 16, 128)

    decode_step(0)
    pass_step(2)
    decode_step(1)
    decode_step(2)
    project_step(3)
    decode_step(3)

    def each_message(do_far, do_near):
        def one(i, c):
            d = lax.div(t, 2) * 32 + lax.rem(t, 2) * 16 + lax.rem(i, 16)
            dest_t = lax.div(i, 16)
            src = dfin.at[lax.rem(i, 16)]
            dst = dec_ref.at[:, pl.ds(pl.multiple_of(dp * 128, 128), 128)]
            near = jnp.logical_and(d == dp, dest_t == t)

            @pl.when(near)
            def _():
                if do_near:
                    do_near(pltpu.make_async_copy(src, dst, out_r.at[0]))

            @pl.when(jnp.logical_not(near))
            def _():
                do_far(pltpu.make_async_remote_copy(
                    src_ref=src, dst_ref=dst, send_sem=out_s.at[i], recv_sem=out_r.at[0],
                    device_id=(d, dest_t), device_id_type=MESH))

            return c

        lax.fori_loop(0, 64, one, 0)

    each_message(lambda c: c.start(), lambda c: c.start())
    pass_step(3)
    for k in (3, 1, 2):
        rot_copy(k).wait()
    pltpu.make_async_copy(dec_ref, dec_ref, out_r.at[0]).wait()
    each_message(lambda c: c.wait_send(), None)
    for k in range(4):
        for step in range(3):
            rs_copy(k, step).wait_send()
    for y_lo in range(2):
        for step in range(3):
            ds_copy(y_lo, step).wait_send()
    gath_w.end()
    gath_h.end()


def exchange(pick, heads, out_proj, resp_act, gain, wt):
    width = wt.shape[1]
    vmem = pl.BlockSpec(memory_space=pltpu.VMEM)
    dma = pltpu.SemaphoreType.DMA
    return pl.pallas_call(
        kernel,
        out_shape=(
            jax.ShapeDtypeStruct((16, 8192), BF16),
            jax.ShapeDtypeStruct((512, 512), BF16),
        ),
        in_specs=[vmem] * 6,
        out_specs=(vmem, vmem),
        scratch_shapes=[
            pltpu.VMEM((2, 4, 4, 2, 2, 32, width // 2), BF16),
            pltpu.VMEM((2, 4, 4, 2, 2, 16, width), BF16),
            pltpu.VMEM((512, width), BF16),
            pltpu.VMEM((512, 512), F32),
            pltpu.VMEM((4, 4, 128, 512), BF16),
            pltpu.VMEM((4, 3, 128, 512), BF16),
            pltpu.VMEM((8, 128, 128), F32),
            pltpu.VMEM((2, 3, 128, 128), BF16),
            pltpu.VMEM((2, 3, 128, 128), BF16),
            pltpu.VMEM((16, 16, 128), BF16),
            pltpu.VMEM((4, 8, 128), F32),
            pltpu.VMEM((3, 4, 8, 128), F32),
            dma((2, 32)), dma((2, 32)), dma((2,)),
            dma((2, 32)), dma((2, 32)), dma((2,)),
            dma((4, 3)), dma((4, 3)), dma((2, 3)), dma((2, 3)),
            dma((3,)), dma((3,)), dma((4,)), dma((4,)), dma((64,)), dma((1,)),
        ],
        compiler_params=pltpu.CompilerParams(
            collective_id=0, has_side_effects=True, vmem_limit_bytes=56 * 1024 * 1024),
    )(pick, heads, out_proj, resp_act, gain, wt)


def attend(queries, fresh_kv, kv_cache, cache_len):
    steps, layers, rows, width = queries.shape
    cache = kv_cache.shape[2]
    kvs = kv_cache.shape[-1] // HEAD
    group = width // (kvs * HEAD)
    scale = 1.0 / math.sqrt(HEAD)
    q = queries.reshape(steps, layers, rows, kvs, group, HEAD)
    c = kv_cache.reshape(layers, rows, cache, 2, kvs, HEAD)
    f = fresh_kv.reshape(steps, layers, rows, 2, kvs, HEAD)
    cs = jnp.einsum("slrkgd,lrpkd->lrksgp", q, c[:, :, :, 0], preferred_element_type=jnp.float32) * scale
    fs = jnp.einsum("slrkgd,ulrkd->lrksgu", q, f[:, :, :, 0], preferred_element_type=jnp.float32) * scale
    valid = jnp.arange(cache, dtype=jnp.int32)[None, :] < cache_len[:, None]
    cs = jnp.where(valid[None, :, None, None, None, :], cs, masked_score)
    order = jnp.arange(steps, dtype=jnp.int32)
    seen = order[None, :] <= order[:, None]
    fs = jnp.where(seen[None, None, None, :, None, :], fs, masked_score)
    peak = jnp.maximum(cs.max(-1), fs.max(-1))[..., None]
    ce = jnp.exp(cs - peak)
    fe = jnp.exp(fs - peak)
    total = ce.sum(-1, keepdims=True) + fe.sum(-1, keepdims=True)
    cw = (ce / total).astype(jnp.bfloat16)
    fw = (fe / total).astype(jnp.bfloat16)
    out = jnp.einsum("lrksgp,lrpkd->srlkgd", cw, c[:, :, :, 1], preferred_element_type=jnp.float32)
    out = out + jnp.einsum("lrksgu,ulrkd->srlkgd", fw, f[:, :, :, 1], preferred_element_type=jnp.float32)
    return out.astype(jnp.bfloat16).reshape(steps * rows, layers * width)


def pick_matrix(finished, resp_len, start_shard):
    place = jnp.arange(SPREAD * QUART, dtype=jnp.int32)
    block = jnp.mod(place[None, :] // QUART - start_shard[:, None], SPREAD)
    source = block * QUART + place[None, :] % QUART
    live = (finished[:, None] == 1) & (source < resp_len[:, None])
    return ((source[:, :, None] == place) & live[:, :, None]).astype(BF16)


def shards(
    queries,
    fresh_kv,
    kv_cache,
    cache_len,
    out_proj,
    finished,
    resp_len,
    start_shard,
    resp_act,
    reward_gain,
    reward_weight,
):
    steps, layers, rows, width = queries.shape
    heads = attend(queries, fresh_kv, kv_cache, cache_len)
    pick = pick_matrix(finished, resp_len, start_shard)
    dec, scored = exchange(
        pick, heads, out_proj, resp_act, reward_gain.reshape(1, -1), reward_weight.T
    )
    return dec.reshape(steps, rows, -1), scored


def solution(mesh):
    return jax.shard_map(
        shards,
        mesh=mesh,
        in_specs=(
            P(None, None, "dp", "tensor"),
            P(None, None, "dp", None, "tensor"),
            P(None, "dp", None, None, "tensor"),
            P("dp"),
            P(None, "tensor", "dp"),
            P("dp"),
            P("dp"),
            P("dp"),
            P("dp", None, "tensor"),
            P("tensor"),
            P("tensor", "dp"),
        ),
        out_specs=(P(None, "dp", None), P("dp", "tensor")),
        check_vma=False,
    )
```

time: 385 us -> 149 us (0.39)
  waiting for transfers between devices: 265 us -> 0 us
  Pallas kernels: 0 us -> 120 us
  blocking collectives: 37.9 us -> 0 us
  starting transfers between devices: 14.4 us -> 0 us
  matrix products: 19.2 us -> 5.22 us
  between operations: 13.9 us -> 0.77 us
  other arithmetic: 8.22 us -> 1.62 us
  local copies, waits for them, and re-layouts: 24.7 us -> 20.5 us
    all_gather x2 -> x0, waiting for transfers between devices: 185 us -> none  [the longest x1 110 us: shards(): heads = lax.all_gather(heads, 'dp', axis=0, tiled=True)]
    pallas_call x0 -> x1, Pallas kernels: none -> 120 us  [exchange(): pl.pallas_call(kernel, out_shape=(jax.ShapeDtypeStruct((16, 8192), BF16),...]
    reduce_scatter x1 -> x0, waiting for transfers between devices: 70.4 us -> none  [shards(): lax.psum_scatter(cols, 'tensor', scatter_dimension=1, tiled=True)]
    psum x1 -> x0, blocking collectives: 37.9 us -> none  [shards(): summed = lax.psum(part, 'tensor').astype(jnp.bfloat16)]
    dot_general x4 -> x2, matrix products: 18 us -> 2.4 us  [the longest x1 2.14 us: attend(): jnp.einsum('lrksgp,lrpkd->srlkgd', cw, c[:, :, :, 1], preferred_element_t...]
    ppermute x3 -> x0, waiting for transfers between devices: 9.09 us -> none  [shifted(): return lax.ppermute(block, axis, route)]
    all_to_all x1 -> x0, starting transfers between devices: 7.31 us -> none  [shards(): lax.all_to_all(summed.reshape(groups, rows, steps, -1), 'dp', split_axis=...]
    ppermute x3 -> x0, starting transfers between devices: 7.02 us -> none  [shifted(): return lax.ppermute(block, axis, route)]
  transfers between devices with their start and end apart: 7 -> 0, of which waited for: 5 -> 0; matrix products, arithmetic and copies ran while one was open for 5% -> 0% of each run, Pallas kernels for 0% -> 0%
where the time goes in v2:
time: 149 us; the launch traced here: 148 us
  Pallas kernels  120 us (81%)
  local copies, waits for them, and re-layouts  20.5 us (14%)
  matrix products  5.22 us (4%)
  other arithmetic  1.62 us (1%)
    pallas_call x1, Pallas kernels, exchange(): pl.pallas_call(kernel, out_shape=(jax.ShapeDtypeStruct((16, 8192), BF16),...  120 us
    unnamed x17, local copies, waits for them, and re-layouts  15.4 us

profile of v2, /device:TPU:1, one launch (start us, length us, event | category | flops | bytes accessed | tf_op | source)
XLA Modules:
  0.0 148.3 jit_solution(16174782976192980201)
XLA Ops:
  0.6 0.0 copy-start
  0.6 0.0 copy-start.4
  0.6 11.2 %copy.20 = bf16[2,4,512,2,256]{2,4,3,1,0:T(8,128)(2,1)} copy(bf16[2,4,512,2,256]{4,3,2,1,0:T(2,128)(2,1)} %param.13) | data formatting | bytes 8388608 | tf_op args[2]
  11.8 0.0 copy-start.1
  11.8 0.0 copy-done
  11.8 0.1 reshape.238
  11.9 0.0 copy-done.4
  11.9 0.1 iota_compare_fusion.1
  12.0 2.1 %fusion.28 = (f32[2,4,2,4,8]{4,3,2,1,0:T(4,128)S(1)}, f32[2,4,2,4,8,512]{5,4,3,2,1,0:T(8,128)S(1)}) fusion(bf16[2,4,512,2,2,128]{2,5,4,3,1,0:T(8,128)(2,1)} %bitcast.45, bf16[4,2,4,2,8,128]{5,4,3,2,1,0:T(8,128)(2,1)S(1)} %reshape.238, pred[4,512]{1,0:T(4,128)(4,1)S(1)} %iota_compare_fusion.1), kind=kOutput, calls=%fused_computation.45 | convolution fusion | flops 67894784 | bytes 3280896 | tf_op jit(solution)/shard_map/slrkgd,lrpkd->lrksgp/dot_general | solution.py:448
  14.1 0.0 copy-done.1
  14.2 0.7 fusion.29
  14.9 0.1 fusion.21
  15.1 0.3 fusion.15
  15.5 0.3 fusion.22
  15.7 1.8 %slice.18 = bf16[2,4,512,1,2,128]{2,5,4,3,1,0:T(8,128)(2,1)S(1)} slice(bf16[2,4,512,2,2,128]{2,5,4,3,1,0:T(8,128)(2,1)} %bitcast.46), slice={[0:2], [0:4], [0:512], [1:2], [0:2], [0:128]} | slice | bytes 4194304 | tf_op jit(solution)/shard_map/slice | solution.py:461
  17.5 2.4 %copy.36 = bf16[2,4,512,1,2,128]{5,2,4,0,1,3:T(8,128)(2,1)} copy(bf16[2,4,512,1,2,128]{2,5,4,3,1,0:T(8,128)(2,1)S(1)} %slice.18) | data formatting | bytes 4194304
  19.9 0.0 copy-start.6
  19.9 0.0 copy-start.3
  19.9 0.0 copy-start.5
  19.9 0.0 copy-start.2
  19.9 2.1 %fusion.11 = bf16[4,4,2,2,8,128]{5,4,0,3,2,1:T(8,128)(2,1)S(1)} fusion(f32[4,2,2,4,8,128]{5,4,3,2,1,0:T(8,128)S(1)} %fusion.22, bf16[2,4,512,1,2,128]{5,2,4,0,1,3:T(8,128)(2,1)} %copy.36, f32[2,4,2,4,8,512]{5,4,3,2,1,0:T(8,128)S(1)} %get-tuple-element.9, f32[2,4,2,4,8]{4,3,2,1,0:T(4,128)S(1)} %add.61, f32[2,4,2,4,8]{4,3,2,1,0:T(4,128)S(1)} %max.7), kind=kOutput, calls=%fused_computation.8 | convolution fusion | flops 68026368 | bytes 3543040 | tf_op jit(solution)/shard_map/lrksgp,lrpkd->srlkgd/dot_general | solution.py:461
  22.1 0.7 reshape.241.heads_ref
  22.8 0.0 copy-done.6
  22.8 0.0 copy-done.3
  22.8 0.0 copy-done.5
  22.8 0.1 compare_and_fusion
  22.9 0.1 fusion.25
  23.0 0.9 fusion.18.pick_ref
  23.9 0.0 copy-done.2
  23.9 0.6 reshape.242.gain_ref
  24.5 120.2 %shard_map.122 = (bf16[16,8192]{1,0:T(8,128)(2,1)}, bf16[512,512]{1,0:T(8,128)(2,1)}) custom-call(bf16[4,128,128]{2,1,0:T(8,128)(2,1)} %fusion.18.pick_ref, bf16[16,4096]{1,0:T(8,128)(2,1)} %reshape.241.heads_ref, bf16[2,2048,128]{2,1,0:T(8,128)(2,1)} %outp_ref.1, bf16[4,128,2048]{2,1,0:T(8,128)(2,1)} %resp_ref.1, bf16[1,2048]{1,0:T(2,128)(2,1)} %reshape.242.gain_ref, ...), custom_call_target="tpu_custom_call" | custom-call | tf_op jit(solution)/shard_map/pallas_call | solution.py:408
  144.7 1.8 %reshape.243 = bf16[4,4,8192]{2,1,0:T(4,128)(2,1)} reshape(bf16[16,8192]{1,0:T(8,128)(2,1)} %get-tuple-element.4) | data formatting | bytes 524288 | tf_op jit(solution)/shard_map/reshape | solution.py:493
  146.4 1.9 %copy.57 = bf16[512,512]{1,0:T(8,128)(2,1)} copy(bf16[512,512]{1,0:T(8,128)(2,1)} %get-tuple-element.17) | data formatting | bytes 1048576
  (8 shorter events, 0.1 us)
Async XLA Ops:
  0.6 11.2 %copy-start = (bf16[4,2,4,2048]{3,2,1,0:T(4,128)(2,1)S(1)}, bf16[4,2,4,2048]{3,2,1,0:T(4,128)(2,1)}, u32[]{:S(2)}) copy-start(bf16[4,2,4,2048]{3,2,1,0:T(4,128)(2,1)} %param.11) | copy-start | bytes 393220
  0.6 11.3 %copy-start.4 = (s32[4]{0:T(128)S(1)}, s32[4]{0:T(128)}, u32[]{:S(2)}) copy-start(s32[4]{0:T(128)} %param.14) | copy-start | bytes 52
  11.8 2.3 %copy-start.1 = (bf16[4,2,4,2,256]{4,3,2,1,0:T(2,128)(2,1)S(1)}, bf16[4,2,4,2,256]{4,3,2,1,0:T(2,128)(2,1)}, u32[]{:S(2)}) copy-start(bf16[4,2,4,2,256]{4,3,2,1,0:T(2,128)(2,1)} %param.12) | copy-start | bytes 98308
  19.9 2.9 %copy-start.6 = (s32[4]{0:T(128)S(1)}, s32[4]{0:T(128)}, u32[]{:S(2)}) copy-start(s32[4]{0:T(128)} %param.16) | copy-start | bytes 52
  19.9 2.9 %copy-start.3 = (s32[4]{0:T(128)S(1)}, s32[4]{0:T(128)}, u32[]{:S(2)}) copy-start(s32[4]{0:T(128)} %param.18) | copy-start | bytes 52
  19.9 2.9 %copy-start.5 = (s32[4]{0:T(128)S(1)}, s32[4]{0:T(128)}, u32[]{:S(2)}) copy-start(s32[4]{0:T(128)} %param.17) | copy-start | bytes 52
  19.9 4.0 %copy-start.2 = (bf16[2048]{0:T(1024)(128)(2,1)S(1)}, bf16[2048]{0:T(1024)(128)(2,1)}, u32[]{:S(2)}) copy-start(bf16[2048]{0:T(1024)(128)(2,1)} %param.20) | copy-start | bytes 12292

commit v3 on v2

--- a/solution.py
+++ b/solution.py
@@ -165,11 +165,11 @@
 
 
 def kernel(
-    pick_ref, heads_ref, outp_ref, resp_ref, gain_ref, wt_ref,
+    meta_ref, q_ref, fresh_ref, gain_ref, kv_hbm, outp_hbm, resp_hbm, wt_ref,
     dec_ref, scored_ref,
-    gw, gh, normed, pacc, rs_send, rs_recv, dacc, ds_send, ds_recv, dfin, sq_own, sq_got,
+    kv_ref, outp_ref, resp_ref, q_rows, heads_ref, by_row, gw, gh, normed, pacc, rs_send, rs_recv, dacc, ds_send, ds_recv, dfin, sq_own, sq_got,
     w_send, w_recv, w_local, h_send, h_recv, h_local,
-    rss, rsr, dss, dsr, sqs, sqr, rot_s, rot_r, out_s, out_r,
+    rss, rsr, dss, dsr, sqs, sqr, rot_s, rot_r, out_s, out_r, in_s,
 ):
     p = Place()
     dp, t = p.dp, p.t
@@ -178,6 +178,13 @@
     half_w = width // 2
     is_self = lax.div(dp, 16) == t
 
+    resp_in = pltpu.make_async_copy(resp_hbm, resp_ref, in_s.at[0])
+    kv_in = pltpu.make_async_copy(kv_hbm, kv_ref, in_s.at[1])
+    outp_in = pltpu.make_async_copy(outp_hbm, outp_ref, in_s.at[2])
+    resp_in.start()
+    kv_in.start()
+    outp_in.start()
+
     barrier = pltpu.get_barrier_semaphore()
 
     def greet(dev):
@@ -206,15 +213,21 @@
     gath_w = Gather(p, lambda h: wt_ref.at[:, pl.ds(h * half_w, half_w)], gw, w_send, w_recv, w_local)
     gath_h = Gather(p, lambda h: heads_ref.at[:, pl.ds(h * width, width)], gh, h_send, h_recv, h_local)
     gath_w.start()
-    gath_h.start()
 
     eye = eye_mask()
 
+    row_no = lax.broadcasted_iota(jnp.int32, (128, 128), 0)
+    col_no = lax.broadcasted_iota(jnp.int32, (128, 128), 1)
+
     def turn_rows(r, c):
+        block_no = jnp.bitwise_and(row_no // QUART - meta_ref[3, pl.ds(r, 1), :], SPREAD - 1)
+        source = block_no * QUART + jnp.bitwise_and(row_no, QUART - 1)
+        live = jnp.logical_and(source < meta_ref[2, pl.ds(r, 1), :], meta_ref[1, pl.ds(r, 1), :] == 1)
+        pick = jnp.where(jnp.logical_and(source == col_no, live), 1.0, 0.0).astype(BF16)
         col = jnp.zeros((128, 1), F32)
         for part in range(4):
             cols = slice(part * (width // 4), (part + 1) * (width // 4))
-            block = jnp.dot(pick_ref[r], resp_ref[r, :, cols], preferred_element_type=F32)
+            block = jnp.dot(pick, resp_ref[r, :, cols], preferred_element_type=F32)
             for k in range(SPREAD):
                 normed[pl.ds(pl.multiple_of(k * 128 + r * QUART, QUART), QUART), cols] = block[
                     k * QUART:(k + 1) * QUART].astype(BF16)
@@ -222,6 +235,7 @@
         sq_own[r] = jnp.broadcast_to(jnp.sum(jnp.where(eye, col, 0.0), axis=0, keepdims=True), (8, 128))
         return c
 
+    resp_in.wait()
     lax.fori_loop(0, ROWS_G, turn_rows, 0)
 
     def sq_copy(d):
@@ -232,9 +246,7 @@
     for d in (1, 2, 3):
         sq_copy(d).start()
 
-    gath_w.after_z()
-    for d in (1, 2, 3):
-        sq_copy(d).wait()
+    gain = jnp.concatenate([gain_ref[i:i + 1, :].astype(F32) for i in range(width // 128)], axis=1)
 
     def norm_rows(r, c):
         total = sq_own[r] + sq_got[0, r] + sq_got[1, r] + sq_got[2, r]
@@ -242,20 +254,72 @@
         col = jnp.sum(jnp.where(eye, scale, 0.0), axis=1, keepdims=True)
         for k in range(SPREAD):
             rows = pl.ds(pl.multiple_of(k * 128 + r * QUART, QUART), QUART)
-            block = normed[rows, :].astype(F32) * col[k * QUART:(k + 1) * QUART] * gain_ref[...].astype(F32)
+            block = normed[rows, :].astype(F32) * col[k * QUART:(k + 1) * QUART] * gain
             normed[rows, :] = block.astype(BF16)
         return c
 
+    scale_q = 1.0 / math.sqrt(HEAD)
+    fresh_no = lax.broadcasted_iota(jnp.int32, (32, 8), 1)
+    seen = jnp.logical_and(fresh_no % 2 == 0, fresh_no // 2 <= lax.broadcasted_iota(jnp.int32, (32, 8), 0) // 8)
+    cache_no = lax.broadcasted_iota(jnp.int32, (1, 1024), 1)
+
+    def order_queries(layer):
+        for head in range(2):
+            for step in range(4):
+                for g in range(8):
+                    begin = (head * 8 + g) * HEAD
+                    q_rows[layer * 2 + head, pl.ds(step * 8 + g, 4, stride=32), :] = q_ref[
+                        step, layer, :, begin:begin + HEAD].astype(F32)
+
+    def attend_row(layer, head, r):
+        q = q_rows[layer * 2 + head, r * 32:(r + 1) * 32, :]
+        both = kv_ref[layer, r, :, :, head * HEAD:(head + 1) * HEAD].reshape(1024, HEAD)
+        new = fresh_ref[:, layer, r, :, head * HEAD:(head + 1) * HEAD].astype(F32).reshape(8, HEAD)
+        valid = jnp.logical_and(cache_no % 2 == 0, cache_no < 2 * meta_ref[0, r:r + 1, 0:1])
+        cs = jnp.where(valid, dot_nt(q.astype(BF16), both) * scale_q, masked_score)
+        fs = jnp.where(seen, dot_nt(q, new) * scale_q, masked_score)
+        peak = jnp.maximum(jnp.max(cs, axis=1, keepdims=True), jnp.max(fs, axis=1, keepdims=True))
+        ce = jnp.exp(cs - peak)
+        fe = jnp.exp(fs - peak)
+        total = jnp.sum(ce, axis=1, keepdims=True) + jnp.sum(fe, axis=1, keepdims=True)
+        cw = pltpu.roll(ce / total, 1, 1).astype(BF16)
+        fw = (fe / total).astype(BF16).astype(F32)
+        res = jnp.dot(cw, both, preferred_element_type=F32)
+        res = res + jnp.dot(fw, pltpu.roll(new, 7, 0), preferred_element_type=F32)
+        for step in range(4):
+            by_row[(step * 4 + r) * 8:(step * 4 + r + 1) * 8, :] = res[step * 8:(step + 1) * 8]
+
+    def attend_end(layer, head):
+        for g in range(8):
+            begin = layer * width + head * 8 * HEAD + g * HEAD
+            heads_ref[:, begin:begin + HEAD] = by_row[pl.ds(g, 16, stride=8), :].astype(BF16)
+
+    order_queries(0)
+    order_queries(1)
+    gath_w.after_z()
+    kv_in.wait()
+    events = {
+        1: lambda: gath_w.after_first(1),
+        2: lambda: gath_w.after_first(2),
+        4: lambda: gath_w.after_first(3),
+        6: lambda: gath_w.after_second(0),
+        8: lambda: gath_w.after_second(1),
+        10: lambda: gath_w.after_second(2),
+        12: lambda: gath_w.after_second(3),
+        14: lambda: gath_w.after_onward(0),
+    }
+    for u in range(16):
+        attend_row(u // 8, (u // 4) % 2, u % 4)
+        if u % 4 == 3:
+            attend_end(u // 8, (u // 4) % 2)
+        if u in events:
+            events[u]()
+    gath_h.start()
+    for d in (1, 2, 3):
+        sq_copy(d).wait()
     lax.fori_loop(0, ROWS_G, norm_rows, 0)
-
+    gath_h.after_z()
     for i in (1, 2, 3):
-        gath_w.after_first(i)
-    gath_h.after_z()
-    for i in range(4):
-        gath_w.after_second(i)
-    for i in (1, 2, 3):
-        gath_h.after_first(i)
-    for i in range(4):
         gath_w.after_onward(i)
     gath_w.after_across()
 
@@ -314,10 +378,14 @@
 
     project_step(0)
     pass_step(0)
-    for i in range(4):
+    for i in (1, 2, 3):
+        gath_h.after_first(i)
+    for i in range(2):
         gath_h.after_second(i)
     project_step(1)
     pass_step(1)
+    for i in range(2, 4):
+        gath_h.after_second(i)
     for i in range(4):
         gath_h.after_onward(i)
     project_step(2)
@@ -331,36 +399,27 @@
         return (jnp.dot(ha, outp_ref[0], preferred_element_type=F32)
                 + jnp.dot(hb, outp_ref[1], preferred_element_type=F32))
 
-    def decode_tiles(i, c):
-        dacc[i] = decode_part(lax.div(i, 2), lax.rem(i, 2))
-        return c
-
-    lax.fori_loop(0, 8, decode_tiles, 0)
-
-    def ds_copy(y_lo, step):
+    def ds_copy(d):
         return pltpu.make_async_remote_copy(
-            src_ref=ds_send.at[y_lo, step], dst_ref=ds_recv.at[y_lo, step], send_sem=dss.at[y_lo, step],
-            recv_sem=dsr.at[y_lo, step], device_id=(dp, wrap(t + (1 if y_lo else -1), 4)), device_id_type=MESH)
-
-    def decode_step(step):
+            src_ref=ds_send.at[d - 1], dst_ref=ds_recv.at[3 - d], send_sem=dss.at[d - 1], recv_sem=dsr.at[3 - d],
+            device_id=(dp, wrap(t + d, 4)), device_id_type=MESH)
+
+    outp_in.wait()
+    for d in (2, 1, 3):
         for y_lo in range(2):
-            owner = wrap(t - (1 + step) * (1 if y_lo else -1), 4)
-            total = dacc[owner * 2 + y_lo]
-            if step:
-                ds_copy(y_lo, step - 1).wait_recv()
-                total = total + ds_recv[y_lo, step - 1].astype(F32)
-            if step < 3:
-                ds_send[y_lo, step] = total.astype(BF16)
-                ds_copy(y_lo, step).start()
-            else:
-                dfin[pl.ds(y_lo * 8, 8)] = total.astype(BF16).reshape(8, 16, 128)
-
-    decode_step(0)
+            ds_send[d - 1, y_lo * 128:(y_lo + 1) * 128] = decode_part(wrap(t + d, 4), y_lo).astype(BF16)
+        ds_copy(d).start()
+    for y_lo in range(2):
+        dacc[y_lo] = decode_part(t, y_lo)
     pass_step(2)
-    decode_step(1)
-    decode_step(2)
     project_step(3)
-    decode_step(3)
+    for d in (1, 2, 3):
+        ds_copy(d).wait_recv()
+    for y_lo in range(2):
+        total = dacc[y_lo]
+        for d in range(3):
+            total = total + ds_recv[d, y_lo * 128:(y_lo + 1) * 128].astype(F32)
+        dfin[pl.ds(y_lo * 8, 8)] = total.astype(BF16).reshape(8, 16, 128)
 
     def each_message(do_far, do_near):
         def one(i, c):
@@ -394,14 +453,13 @@
     for k in range(4):
         for step in range(3):
             rs_copy(k, step).wait_send()
-    for y_lo in range(2):
-        for step in range(3):
-            ds_copy(y_lo, step).wait_send()
+    for d in (1, 2, 3):
+        ds_copy(d).wait_send()
     gath_w.end()
     gath_h.end()
 
 
-def exchange(pick, heads, out_proj, resp_act, gain, wt):
+def exchange(meta, q, fresh, gain, kv_cache, out_proj, resp_act, wt):
     width = wt.shape[1]
     vmem = pl.BlockSpec(memory_space=pltpu.VMEM)
     dma = pltpu.SemaphoreType.DMA
@@ -411,64 +469,35 @@
             jax.ShapeDtypeStruct((16, 8192), BF16),
             jax.ShapeDtypeStruct((512, 512), BF16),
         ),
-        in_specs=[vmem] * 6,
+        in_specs=[vmem] * 4 + [pl.BlockSpec(memory_space=pl.ANY)] * 4,
         out_specs=(vmem, vmem),
         scratch_shapes=[
+            pltpu.VMEM(kv_cache.shape, BF16),
+            pltpu.VMEM(out_proj.shape, BF16),
+            pltpu.VMEM(resp_act.shape, BF16),
+            pltpu.VMEM((4, 128, 128), F32),
+            pltpu.VMEM((16, 2 * width), BF16),
+            pltpu.VMEM((128, 128), F32),
             pltpu.VMEM((2, 4, 4, 2, 2, 32, width // 2), BF16),
             pltpu.VMEM((2, 4, 4, 2, 2, 16, width), BF16),
             pltpu.VMEM((512, width), BF16),
             pltpu.VMEM((512, 512), F32),
             pltpu.VMEM((4, 4, 128, 512), BF16),
             pltpu.VMEM((4, 3, 128, 512), BF16),
-            pltpu.VMEM((8, 128, 128), F32),
-            pltpu.VMEM((2, 3, 128, 128), BF16),
-            pltpu.VMEM((2, 3, 128, 128), BF16),
+            pltpu.VMEM((2, 128, 128), F32),
+            pltpu.VMEM((3, 256, 128), BF16),
+            pltpu.VMEM((3, 256, 128), BF16),
             pltpu.VMEM((16, 16, 128), BF16),
             pltpu.VMEM((4, 8, 128), F32),
             pltpu.VMEM((3, 4, 8, 128), F32),
             dma((2, 32)), dma((2, 32)), dma((2,)),
             dma((2, 32)), dma((2, 32)), dma((2,)),
-            dma((4, 3)), dma((4, 3)), dma((2, 3)), dma((2, 3)),
-            dma((3,)), dma((3,)), dma((4,)), dma((4,)), dma((64,)), dma((1,)),
+            dma((4, 3)), dma((4, 3)), dma((3,)), dma((3,)),
+            dma((3,)), dma((3,)), dma((4,)), dma((4,)), dma((64,)), dma((1,)), dma((3,)),
         ],
         compiler_params=pltpu.CompilerParams(
             collective_id=0, has_side_effects=True, vmem_limit_bytes=56 * 1024 * 1024),
-    )(pick, heads, out_proj, resp_act, gain, wt)
-
-
-def attend(queries, fresh_kv, kv_cache, cache_len):
-    steps, layers, rows, width = queries.shape
-    cache = kv_cache.shape[2]
-    kvs = kv_cache.shape[-1] // HEAD
-    group = width // (kvs * HEAD)
-    scale = 1.0 / math.sqrt(HEAD)
-    q = queries.reshape(steps, layers, rows, kvs, group, HEAD)
-    c = kv_cache.reshape(layers, rows, cache, 2, kvs, HEAD)
-    f = fresh_kv.reshape(steps, layers, rows, 2, kvs, HEAD)
-    cs = jnp.einsum("slrkgd,lrpkd->lrksgp", q, c[:, :, :, 0], preferred_element_type=jnp.float32) * scale
-    fs = jnp.einsum("slrkgd,ulrkd->lrksgu", q, f[:, :, :, 0], preferred_element_type=jnp.float32) * scale
-    valid = jnp.arange(cache, dtype=jnp.int32)[None, :] < cache_len[:, None]
-    cs = jnp.where(valid[None, :, None, None, None, :], cs, masked_score)
-    order = jnp.arange(steps, dtype=jnp.int32)
-    seen = order[None, :] <= order[:, None]
-    fs = jnp.where(seen[None, None, None, :, None, :], fs, masked_score)
-    peak = jnp.maximum(cs.max(-1), fs.max(-1))[..., None]
-    ce = jnp.exp(cs - peak)
-    fe = jnp.exp(fs - peak)
-    total = ce.sum(-1, keepdims=True) + fe.sum(-1, keepdims=True)
-    cw = (ce / total).astype(jnp.bfloat16)
-    fw = (fe / total).astype(jnp.bfloat16)
-    out = jnp.einsum("lrksgp,lrpkd->srlkgd", cw, c[:, :, :, 1], preferred_element_type=jnp.float32)
-    out = out + jnp.einsum("lrksgu,ulrkd->srlkgd", fw, f[:, :, :, 1], preferred_element_type=jnp.float32)
-    return out.astype(jnp.bfloat16).reshape(steps * rows, layers * width)
-
-
-def pick_matrix(finished, resp_len, start_shard):
-    place = jnp.arange(SPREAD * QUART, dtype=jnp.int32)
-    block = jnp.mod(place[None, :] // QUART - start_shard[:, None], SPREAD)
-    source = block * QUART + place[None, :] % QUART
-    live = (finished[:, None] == 1) & (source < resp_len[:, None])
-    return ((source[:, :, None] == place) & live[:, :, None]).astype(BF16)
+    )(meta, q, fresh, gain, kv_cache, out_proj, resp_act, wt)
 
 
 def shards(
@@ -485,10 +514,10 @@
     reward_weight,
 ):
     steps, layers, rows, width = queries.shape
-    heads = attend(queries, fresh_kv, kv_cache, cache_len)
-    pick = pick_matrix(finished, resp_len, start_shard)
+    meta = jnp.stack([cache_len, finished, resp_len, start_shard])
+    meta = jnp.broadcast_to(meta[:, :, None], (4, rows, 128))
     dec, scored = exchange(
-        pick, heads, out_proj, resp_act, reward_gain.reshape(1, -1), reward_weight.T
+        meta, queries, fresh_kv, reward_gain.reshape(-1, 128), kv_cache, out_proj, resp_act, reward_weight.T
     )
     return dec.reshape(steps, rows, -1), scored
 

time: 149 us -> 116 us (0.78)
  local copies, waits for them, and re-layouts: 20.5 us -> 4.29 us
  Pallas kernels: 120 us -> 110 us
  matrix products: 5.22 us -> 0 us
    unnamed x17 -> x1, local copies, waits for them, and re-layouts: 15.4 us -> 1.87 us
    pallas_call x1, Pallas kernels: 120 us -> 110 us  [exchange(): pl.pallas_call(kernel, out_shape=(jax.ShapeDtypeStruct((16, 8192), BF16),...]
    dot_general x4 -> x0, matrix products: 5.22 us -> none  [the longest x1 2.14 us: attend(): jnp.einsum('lrksgp,lrpkd->srlkgd', cw, c[:, :, :, 1], preferred_element_t...]
    slice x2 -> x0, local copies, waits for them, and re-layouts: 1.82 us -> none  [the longest x1 1.8 us: attend(): c[:, :, :, 1]]
where the time goes in v3:
time: 116 us
  Pallas kernels  110 us (95%)
  local copies, waits for them, and re-layouts  4.29 us (4%)
    pallas_call x1, Pallas kernels, exchange(): pl.pallas_call(kernel, out_shape=(jax.ShapeDtypeStruct((16, 8192), BF16),...  110 us

profile of v3, /device:TPU:1, one launch (start us, length us, event | category | flops | bytes accessed | tf_op | source)
XLA Modules:
  0.0 116.0 jit_solution(11186324980668970912)
XLA Ops:
  0.6 0.7 pad_add_fusion
  1.3 0.7 broadcast_in_dim.2.meta_ref
  2.0 110.3 %shard_map.122 = (bf16[16,8192]{1,0:T(8,128)(2,1)}, bf16[512,512]{1,0:T(8,128)(2,1)}) custom-call(s32[4,4,128]{2,1,0:T(4,128)} %broadcast_in_dim.2.meta_ref, bf16[4,2,4,2048]{3,2,1,0:T(4,128)(2,1)} %q_ref.1, bf16[4,2,4,2,256]{4,3,2,1,0:T(2,128)(2,1)} %fresh_ref.1, bf16[16,128]{1,0:T(8,128)(2,1)} %bitcast.7, bf16[2,4,512,2,256]{4,3,2,1,0:T(2,128)(2,1)} %kv_hbm.1, ...), custom_call_target="tpu_custom_call" | custom-call | tf_op jit(solution)/shard_map/pallas_call | solution.py:466
  112.4 1.8 %reshape.12 = bf16[4,4,8192]{2,1,0:T(4,128)(2,1)} reshape(bf16[16,8192]{1,0:T(8,128)(2,1)} %get-tuple-element.4) | data formatting | bytes 524288 | tf_op jit(solution)/shard_map/reshape | solution.py:522
  114.1 1.9 %copy.14 = bf16[512,512]{1,0:T(8,128)(2,1)} copy(bf16[512,512]{1,0:T(8,128)(2,1)} %get-tuple-element.9) | data formatting | bytes 1048576

commit v4 on v3

--- a/solution.py
+++ b/solution.py
@@ -19,7 +19,8 @@
 
 MESH = pl.DeviceIdType.MESH
 STEP_OFF = (0, 1, -1, 2)
-BACK = {1: 2, -1: 1, 2: 3}
+BACK = {1: 2, -1: 1}
+Z, NEAR, FAR, SECOND, ONWARD, ACROSS = range(6)
 F32 = jnp.float32
 BF16 = jnp.bfloat16
 
@@ -42,8 +43,9 @@
 
 
 class Gather:
-    def __init__(self, place, own, out, send, recv, local):
-        self.p, self.own, self.out, self.send, self.recv, self.local = place, own, out, send, recv, local
+    def __init__(self, place, own, out, send, recv, cross, local):
+        self.p, self.own, self.out, self.send, self.recv = place, own, out, send, recv
+        self.cross, self.local = cross, local
 
     def ring(self, h):
         return (self.p.y, self.p.x) if h == 0 else (self.p.x, self.p.y)
@@ -62,12 +64,13 @@
 
     def copy(self, h, src, dst, send, recv, dev):
         return pltpu.make_async_remote_copy(
-            src_ref=src, dst_ref=dst, send_sem=self.send.at[h, send], recv_sem=self.recv.at[h, recv],
+            src_ref=src, dst_ref=dst, send_sem=self.send.at[send],
+            recv_sem=self.cross.at[0] if send == ACROSS else self.recv.at[h, recv],
             device_id=dev, device_id_type=MESH)
 
     def z_copy(self, h):
         s, f = self.ring(h)
-        return self.copy(h, self.own(h), self.out.at[h, s, f, self.p.zl, self.p.core], 0, 0,
+        return self.copy(h, self.own(h), self.out.at[h, s, f, self.p.zl, self.p.core], Z, 0,
                          self.dev(h, s, f, zl=1 - self.p.zl))
 
     def own_copy(self, h):
@@ -82,36 +85,40 @@
     def first(self, h, i):
         s, f = self.ring(h)
         u = self.unit(h, 0)
-        return self.copy(h, u, u, i, BACK[STEP_OFF[i]], self.dev(h, s, wrap(f + STEP_OFF[i], 4)))
+        return self.copy(h, u, u, NEAR, BACK[STEP_OFF[i]], self.dev(h, s, wrap(f + STEP_OFF[i], 4)))
+
+    def far(self, h, i):
+        s, f = self.ring(h)
+        u = self.out.at[h, s, wrap(f + STEP_OFF[i], 4), i - 1, self.p.core]
+        return self.copy(h, u, u, FAR, 3 if i == 1 else 16, self.dev(h, s, wrap(f - STEP_OFF[i], 4)))
 
     def second(self, h, i, right):
         s, f = self.ring(h)
         u = self.unit(h, i)
-        step = 1 if right else -1
-        base = 8 if right else 4
-        return self.copy(h, u, u, base + i, base + i, self.dev(h, wrap(s + step, 4), f))
+        return self.copy(h, u, u, SECOND, (8 if right else 4) + i, self.dev(h, wrap(s + (1 if right else -1), 4), f))
 
     def onward(self, h, i):
         s, f = self.ring(h)
         u = self.unit(h, (8 if i < 2 else 4) + i)
-        return self.copy(h, u, u, 12 + i, 12 + i, self.dev(h, wrap(s + (1 if i < 2 else -1), 4), f))
+        return self.copy(h, u, u, ONWARD, 12 + i, self.dev(h, wrap(s + (1 if i < 2 else -1), 4), f))
 
     def across(self, h, j):
         s, f = self.ring(h)
         u = self.unit(h, j)
-        return self.copy(h, u, u, 16 + j, 16 + j, self.dev(h, s, f, core=1 - self.p.core))
+        return self.copy(h, u, u, ACROSS, 0, self.dev(h, s, f, core=1 - self.p.core))
+
+    def wait_for(self, h, ref, recv):
+        pltpu.make_async_copy(ref, ref, self.recv.at[h, recv]).wait()
 
     def arrived(self, h, j):
-        u = self.unit(h, j)
-        self.copy(h, u, u, j, j, self.dev(h, *self.ring(h), core=1 - self.p.core)).wait_recv()
+        self.wait_for(h, self.unit(h, j), j)
 
     def after_z(self):
         for h in range(2):
             s, f = self.ring(h)
-            u = self.out.at[h, s, f, 1 - self.p.zl, self.p.core]
-            self.copy(h, u, u, 0, 0, self.dev(h, s, f, zl=1 - self.p.zl)).wait_recv()
+            self.wait_for(h, self.out.at[h, s, f, 1 - self.p.zl, self.p.core], 0)
             self.own_copy(h).wait()
-            for i in (1, 2, 3):
+            for i in (1, 2):
                 self.first(h, i).start()
             for right in (True, False):
                 self.second(h, 0, right).start()
@@ -119,7 +126,13 @@
 
     def after_first(self, i):
         for h in range(2):
-            self.arrived(h, i)
+            if i < 3:
+                self.arrived(h, i)
+                self.far(h, i).start()
+            else:
+                s, f = self.ring(h)
+                for zl in range(2):
+                    self.wait_for(h, self.out.at[h, s, wrap(f + 2, 4), zl, self.p.core], 16 if zl else 3)
             for right in (True, False):
                 self.second(h, i, right).start()
             self.across(h, i).start()
@@ -138,22 +151,20 @@
             self.across(h, 12 + i).start()
 
     def after_across(self):
-        for h in range(2):
-            for j in range(16):
-                u = self.unit(h, j, core=1 - self.p.core)
-                self.copy(h, u, u, 16 + j, 16 + j, self.dev(h, *self.ring(h), core=1 - self.p.core)).wait_recv()
+        u = self.out.at[:, :, :, :, 1 - self.p.core]
+        pltpu.make_async_copy(u, u, self.cross.at[0]).wait()
 
     def end(self):
-        for h in range(2):
-            self.z_copy(h).wait_send()
-            for i in (1, 2, 3):
-                self.first(h, i).wait_send()
-            for i in range(4):
-                self.second(h, i, True).wait_send()
-                self.second(h, i, False).wait_send()
-                self.onward(h, i).wait_send()
-            for j in range(16):
-                self.across(h, j).wait_send()
+        sent = {
+            Z: self.out.at[:, 0, 0, 0, 0],
+            NEAR: self.out.at[:, 0, pl.ds(0, 2), :, 0],
+            FAR: self.out.at[:, 0, 0, :, 0],
+            SECOND: self.out.at[:, pl.ds(0, 2), :, :, 0],
+            ONWARD: self.out.at[:, 0, :, :, 0],
+            ACROSS: self.out.at[:, :, :, :, 0],
+        }
+        for kind, ref in sent.items():
+            pltpu.make_async_copy(ref, ref, self.send.at[kind]).wait()
 
 
 def eye_mask():
@@ -168,7 +179,7 @@
     meta_ref, q_ref, fresh_ref, gain_ref, kv_hbm, outp_hbm, resp_hbm, wt_ref,
     dec_ref, scored_ref,
     kv_ref, outp_ref, resp_ref, q_rows, heads_ref, by_row, gw, gh, normed, pacc, rs_send, rs_recv, dacc, ds_send, ds_recv, dfin, sq_own, sq_got,
-    w_send, w_recv, w_local, h_send, h_recv, h_local,
+    w_send, w_recv, w_cross, w_local, h_send, h_recv, h_cross, h_local,
     rss, rsr, dss, dsr, sqs, sqr, rot_s, rot_r, out_s, out_r, in_s,
 ):
     p = Place()
@@ -178,6 +189,10 @@
     half_w = width // 2
     is_self = lax.div(dp, 16) == t
 
+    def wait_all(ref, sem):
+        pltpu.make_async_copy(ref, ref, sem.at[0]).wait()
+
+
     resp_in = pltpu.make_async_copy(resp_hbm, resp_ref, in_s.at[0])
     kv_in = pltpu.make_async_copy(kv_hbm, kv_ref, in_s.at[1])
     outp_in = pltpu.make_async_copy(outp_hbm, outp_ref, in_s.at[2])
@@ -198,20 +213,10 @@
         greet((dp, wrap(t + d, 4)))
         greet((wrap(dp - d, groups), t))
 
-    def greet_source(d, c):
-        src_t = lax.div(dp, 16)
-
-        @pl.when(jnp.logical_not(jnp.logical_and(d == dp, src_t == t)))
-        def _():
-            greet((d, src_t))
-
-        return c
-
-    lax.fori_loop(0, groups, greet_source, 0)
-    pl.semaphore_wait(barrier, 14 + groups - is_self.astype(jnp.int32))
-
-    gath_w = Gather(p, lambda h: wt_ref.at[:, pl.ds(h * half_w, half_w)], gw, w_send, w_recv, w_local)
-    gath_h = Gather(p, lambda h: heads_ref.at[:, pl.ds(h * width, width)], gh, h_send, h_recv, h_local)
+    pl.semaphore_wait(barrier, 14)
+
+    gath_w = Gather(p, lambda h: wt_ref.at[:, pl.ds(h * half_w, half_w)], gw, w_send, w_recv, w_cross, w_local)
+    gath_h = Gather(p, lambda h: heads_ref.at[:, pl.ds(h * width, width)], gh, h_send, h_recv, h_cross, h_local)
     gath_w.start()
 
     eye = eye_mask()
@@ -235,16 +240,10 @@
         sq_own[r] = jnp.broadcast_to(jnp.sum(jnp.where(eye, col, 0.0), axis=0, keepdims=True), (8, 128))
         return c
 
-    resp_in.wait()
-    lax.fori_loop(0, ROWS_G, turn_rows, 0)
-
     def sq_copy(d):
         return pltpu.make_async_remote_copy(
-            src_ref=sq_own, dst_ref=sq_got.at[3 - d], send_sem=sqs.at[d - 1], recv_sem=sqr.at[3 - d],
+            src_ref=sq_own, dst_ref=sq_got.at[3 - d], send_sem=sqs.at[0], recv_sem=sqr.at[0],
             device_id=(dp, wrap(t + d, 4)), device_id_type=MESH)
-
-    for d in (1, 2, 3):
-        sq_copy(d).start()
 
     gain = jnp.concatenate([gain_ref[i:i + 1, :].astype(F32) for i in range(width // 128)], axis=1)
 
@@ -297,14 +296,18 @@
     order_queries(0)
     order_queries(1)
     gath_w.after_z()
+    resp_in.wait()
+    lax.fori_loop(0, ROWS_G, turn_rows, 0)
+    for d in (1, 2, 3):
+        sq_copy(d).start()
+    gath_w.after_first(1)
+    gath_w.after_first(2)
     kv_in.wait()
     events = {
-        1: lambda: gath_w.after_first(1),
-        2: lambda: gath_w.after_first(2),
-        4: lambda: gath_w.after_first(3),
-        6: lambda: gath_w.after_second(0),
-        8: lambda: gath_w.after_second(1),
-        10: lambda: gath_w.after_second(2),
+        1: lambda: gath_w.after_first(3),
+        3: lambda: gath_w.after_second(0),
+        6: lambda: gath_w.after_second(1),
+        9: lambda: gath_w.after_second(2),
         12: lambda: gath_w.after_second(3),
         14: lambda: gath_w.after_onward(0),
     }
@@ -315,8 +318,8 @@
         if u in events:
             events[u]()
     gath_h.start()
-    for d in (1, 2, 3):
-        sq_copy(d).wait()
+    wait_all(sq_got, sqs)
+    wait_all(sq_got, sqr)
     lax.fori_loop(0, ROWS_G, norm_rows, 0)
     gath_h.after_z()
     for i in (1, 2, 3):
@@ -342,13 +345,13 @@
 
     def rs_copy(k, step):
         return pltpu.make_async_remote_copy(
-            src_ref=rs_send.at[k, step], dst_ref=rs_recv.at[k, step], send_sem=rss.at[k, step],
+            src_ref=rs_send.at[k, step], dst_ref=rs_recv.at[k, step], send_sem=rss.at[0],
             recv_sem=rsr.at[k, step], device_id=(dp, wrap(t + direction(k), 4)), device_id_type=MESH)
 
     def rot_copy(k):
         rows = scored_ref.at[pl.ds(k * 128, 128), :]
         return pltpu.make_async_remote_copy(
-            src_ref=rs_send.at[k, 3], dst_ref=rows, send_sem=rot_s.at[k], recv_sem=rot_r.at[k],
+            src_ref=rs_send.at[k, 3], dst_ref=rows, send_sem=rot_s.at[0], recv_sem=rot_r.at[0],
             device_id=(lax.rem(dp + k, groups), t), device_id_type=MESH)
 
     def project_step(step):
@@ -360,8 +363,8 @@
             project(wrap(t + 1 + step, 4), 0, 256)
             project(wrap(t - 1 - step, 4), 256, 256)
 
-    def pass_step(step):
-        for k in (3, 1, 2, 0):
+    def pass_step(step, ks):
+        for k in ks:
             rows = slice(k * 128, (k + 1) * 128)
             total = pacc[rows, :]
             if step:
@@ -377,18 +380,24 @@
                 rot_copy(k).start()
 
     project_step(0)
-    pass_step(0)
+    pass_step(0, (3, 1, 2, 0))
+    gath_h.after_first(1)
+    gath_h.after_first(2)
+    project_step(1)
+    gath_h.after_first(3)
+    pass_step(1, (3, 1))
+    gath_h.after_second(0)
+    pass_step(1, (2, 0))
+    gath_h.after_second(1)
+    project_step(2)
+    pass_step(2, (3, 1))
+    gath_h.after_second(2)
+    pass_step(2, (2, 0))
+    gath_h.after_second(3)
+    gath_h.after_onward(0)
+    project_step(3)
     for i in (1, 2, 3):
-        gath_h.after_first(i)
-    for i in range(2):
-        gath_h.after_second(i)
-    project_step(1)
-    pass_step(1)
-    for i in range(2, 4):
-        gath_h.after_second(i)
-    for i in range(4):
         gath_h.after_onward(i)
-    project_step(2)
     gath_h.after_across()
 
     def decode_part(owner, y_lo):
@@ -401,7 +410,7 @@
 
     def ds_copy(d):
         return pltpu.make_async_remote_copy(
-            src_ref=ds_send.at[d - 1], dst_ref=ds_recv.at[3 - d], send_sem=dss.at[d - 1], recv_sem=dsr.at[3 - d],
+            src_ref=ds_send.at[d - 1], dst_ref=ds_recv.at[3 - d], send_sem=dss.at[0], recv_sem=dsr.at[0],
             device_id=(dp, wrap(t + d, 4)), device_id_type=MESH)
 
     outp_in.wait()
@@ -411,50 +420,49 @@
         ds_copy(d).start()
     for y_lo in range(2):
         dacc[y_lo] = decode_part(t, y_lo)
-    pass_step(2)
-    project_step(3)
-    for d in (1, 2, 3):
-        ds_copy(d).wait_recv()
+    pass_step(3, (3, 1))
+    wait_all(ds_recv, dsr)
     for y_lo in range(2):
         total = dacc[y_lo]
         for d in range(3):
             total = total + ds_recv[d, y_lo * 128:(y_lo + 1) * 128].astype(F32)
         dfin[pl.ds(y_lo * 8, 8)] = total.astype(BF16).reshape(8, 16, 128)
 
-    def each_message(do_far, do_near):
-        def one(i, c):
-            d = lax.div(t, 2) * 32 + lax.rem(t, 2) * 16 + lax.rem(i, 16)
-            dest_t = lax.div(i, 16)
-            src = dfin.at[lax.rem(i, 16)]
-            dst = dec_ref.at[:, pl.ds(pl.multiple_of(dp * 128, 128), 128)]
-            near = jnp.logical_and(d == dp, dest_t == t)
-
-            @pl.when(near)
-            def _():
-                if do_near:
-                    do_near(pltpu.make_async_copy(src, dst, out_r.at[0]))
-
-            @pl.when(jnp.logical_not(near))
-            def _():
-                do_far(pltpu.make_async_remote_copy(
-                    src_ref=src, dst_ref=dst, send_sem=out_s.at[i], recv_sem=out_r.at[0],
-                    device_id=(d, dest_t), device_id_type=MESH))
-
-            return c
-
-        lax.fori_loop(0, 64, one, 0)
-
-    each_message(lambda c: c.start(), lambda c: c.start())
-    pass_step(3)
-    for k in (3, 1, 2):
-        rot_copy(k).wait()
-    pltpu.make_async_copy(dec_ref, dec_ref, out_r.at[0]).wait()
-    each_message(lambda c: c.wait_send(), None)
-    for k in range(4):
-        for step in range(3):
-            rs_copy(k, step).wait_send()
-    for d in (1, 2, 3):
-        ds_copy(d).wait_send()
+    def send_message(i, c):
+        d = t * 16 + lax.rem(i, 16)
+        dest_t = lax.div(i, 16)
+        src = dfin.at[lax.rem(i, 16)]
+        dst = dec_ref.at[:, pl.ds(pl.multiple_of(dp * 128, 128), 128)]
+        near = jnp.logical_and(d == dp, dest_t == t)
+
+        @pl.when(near)
+        def _():
+            pltpu.make_async_copy(src, dst, out_r.at[0]).start()
+
+        @pl.when(jnp.logical_not(near))
+        def _():
+            pltpu.make_async_remote_copy(
+                src_ref=src, dst_ref=dst, send_sem=out_s.at[0], recv_sem=out_r.at[0],
+                device_id=(d, dest_t), device_id_type=MESH).start()
+
+        return c
+
+    lax.fori_loop(0, 64, send_message, 0)
+    pass_step(3, (2, 0))
+    wait_all(scored_ref.at[pl.ds(128, 384), :], rot_r)
+    wait_all(rs_send.at[pl.ds(1, 3), 3], rot_s)
+    wait_all(dec_ref, out_r)
+
+    @pl.when(is_self)
+    def _():
+        wait_all(dec_ref.at[:, pl.ds(0, 63 * 128)], out_s)
+
+    @pl.when(jnp.logical_not(is_self))
+    def _():
+        wait_all(dec_ref, out_s)
+
+    wait_all(rs_send.at[:, pl.ds(0, 3)], rss)
+    wait_all(ds_send, dss)
     gath_w.end()
     gath_h.end()
 
@@ -490,10 +498,10 @@
             pltpu.VMEM((16, 16, 128), BF16),
             pltpu.VMEM((4, 8, 128), F32),
             pltpu.VMEM((3, 4, 8, 128), F32),
-            dma((2, 32)), dma((2, 32)), dma((2,)),
-            dma((2, 32)), dma((2, 32)), dma((2,)),
-            dma((4, 3)), dma((4, 3)), dma((3,)), dma((3,)),
-            dma((3,)), dma((3,)), dma((4,)), dma((4,)), dma((64,)), dma((1,)), dma((3,)),
+            dma((6,)), dma((2, 17)), dma((1,)), dma((2,)),
+            dma((6,)), dma((2, 17)), dma((1,)), dma((2,)),
+            dma((1,)), dma((4, 3)), dma((1,)), dma((1,)),
+            dma((1,)), dma((1,)), dma((1,)), dma((1,)), dma((1,)), dma((1,)), dma((3,)),
         ],
         compiler_params=pltpu.CompilerParams(
             collective_id=0, has_side_effects=True, vmem_limit_bytes=56 * 1024 * 1024),

time: 116 us -> 110 us (0.948)
  Pallas kernels: 110 us -> 104 us
    pallas_call x1, Pallas kernels: 110 us -> 104 us  [exchange(): pl.pallas_call(kernel, out_shape=(jax.ShapeDtypeStruct((16, 8192), BF16),...]
where the time goes in v4:
time: 110 us
  Pallas kernels  104 us (95%)
  local copies, waits for them, and re-layouts  4.29 us (4%)
    pallas_call x1, Pallas kernels, exchange(): pl.pallas_call(kernel, out_shape=(jax.ShapeDtypeStruct((16, 8192), BF16),...  104 us

profile of v4, /device:TPU:1, one launch (start us, length us, event | category | flops | bytes accessed | tf_op | source)
XLA Modules:
  0.0 109.8 jit_solution(2520734422371443366)
XLA Ops:
  0.6 0.7 pad_add_fusion
  1.3 0.7 broadcast_in_dim.2.meta_ref
  2.0 104.1 %shard_map.122 = (bf16[16,8192]{1,0:T(8,128)(2,1)}, bf16[512,512]{1,0:T(8,128)(2,1)}) custom-call(s32[4,4,128]{2,1,0:T(4,128)} %broadcast_in_dim.2.meta_ref, bf16[4,2,4,2048]{3,2,1,0:T(4,128)(2,1)} %q_ref.1, bf16[4,2,4,2,256]{4,3,2,1,0:T(2,128)(2,1)} %fresh_ref.1, bf16[16,128]{1,0:T(8,128)(2,1)} %bitcast.7, bf16[2,4,512,2,256]{4,3,2,1,0:T(2,128)(2,1)} %kv_hbm.1, ...), custom_call_target="tpu_custom_call" | custom-call | tf_op jit(solution)/shard_map/pallas_call | solution.py:474
  106.1 1.8 %reshape.12 = bf16[4,4,8192]{2,1,0:T(4,128)(2,1)} reshape(bf16[16,8192]{1,0:T(8,128)(2,1)} %get-tuple-element.4) | data formatting | bytes 524288 | tf_op jit(solution)/shard_map/reshape | solution.py:530
  107.9 1.9 %copy.14 = bf16[512,512]{1,0:T(8,128)(2,1)} copy(bf16[512,512]{1,0:T(8,128)(2,1)} %get-tuple-element.9) | data formatting | bytes 1048576

commit v5 on v4

--- a/solution.py
+++ b/solution.py
@@ -79,13 +79,18 @@
 
     def start(self):
         for h in range(2):
+            s, f = self.ring(h)
             self.z_copy(h).start()
             self.own_copy(h).start()
-
-    def first(self, h, i):
-        s, f = self.ring(h)
-        u = self.unit(h, 0)
-        return self.copy(h, u, u, NEAR, BACK[STEP_OFF[i]], self.dev(h, s, wrap(f + STEP_OFF[i], 4)))
+            self.open_rings(h, self.own(h), self.out.at[h, s, f, self.p.zl, self.p.core])
+
+    def open_rings(self, h, src, dst):
+        s, f = self.ring(h)
+        for i in (1, 2):
+            self.copy(h, src, dst, NEAR, BACK[STEP_OFF[i]], self.dev(h, s, wrap(f + STEP_OFF[i], 4))).start()
+        for step, recv in ((1, 8), (-1, 4)):
+            self.copy(h, src, dst, SECOND, recv, self.dev(h, wrap(s + step, 4), f)).start()
+        self.copy(h, src, dst, ACROSS, 0, self.dev(h, s, f, core=1 - self.p.core)).start()
 
     def far(self, h, i):
         s, f = self.ring(h)
@@ -117,12 +122,9 @@
         for h in range(2):
             s, f = self.ring(h)
             self.wait_for(h, self.out.at[h, s, f, 1 - self.p.zl, self.p.core], 0)
+            u = self.out.at[h, s, f, 1 - self.p.zl, self.p.core]
+            self.open_rings(h, u, u)
             self.own_copy(h).wait()
-            for i in (1, 2):
-                self.first(h, i).start()
-            for right in (True, False):
-                self.second(h, 0, right).start()
-            self.across(h, 0).start()
 
     def after_first(self, i):
         for h in range(2):
@@ -329,84 +331,69 @@
     def direction(k):
         return 1 if k >= 2 else -1
 
-    def project(owner, row0, rows):
+    def project(owner, row0):
         zl = lax.div(owner, 2)
-
-        def tile(y_lo, c):
+        rows = pl.ds(row0, 256)
+        for y_lo in range(2):
             y = lax.rem(owner, 2) * 2 + y_lo
             wa = gw[0, y, :, zl].reshape(256, half_w)
             wb = gw[1, :, y, zl].reshape(256, half_w)
-            res = dot_nt(normed[row0:row0 + rows, :half_w], wa)
-            res = res + dot_nt(normed[row0:row0 + rows, half_w:], wb)
-            pacc[row0:row0 + rows, pl.ds(pl.multiple_of(y_lo * 256, 256), 256)] = res
-            return c
-
-        lax.fori_loop(0, 2, tile, 0)
+            pacc[rows, y_lo * 256:(y_lo + 1) * 256] = dot_nt(normed[rows, :half_w], wa) + dot_nt(normed[rows, half_w:], wb)
 
     def rs_copy(k, step):
         return pltpu.make_async_remote_copy(
             src_ref=rs_send.at[k, step], dst_ref=rs_recv.at[k, step], send_sem=rss.at[0],
-            recv_sem=rsr.at[k, step], device_id=(dp, wrap(t + direction(k), 4)), device_id_type=MESH)
+            recv_sem=rsr.at[k, step], device_id=(dp, wrap(t + direction(k) * (1 if step else -1), 4)), device_id_type=MESH)
 
     def rot_copy(k):
-        rows = scored_ref.at[pl.ds(k * 128, 128), :]
         return pltpu.make_async_remote_copy(
-            src_ref=rs_send.at[k, 3], dst_ref=rows, send_sem=rot_s.at[0], recv_sem=rot_r.at[0],
-            device_id=(lax.rem(dp + k, groups), t), device_id_type=MESH)
+            src_ref=rs_send.at[k, 3], dst_ref=scored_ref.at[pl.ds(k * 128, 128), :], send_sem=rot_s.at[0],
+            recv_sem=rot_r.at[0], device_id=(lax.rem(dp + k, groups), t), device_id_type=MESH)
 
     def project_step(step):
-        if step == 1:
-            project(wrap(t + 2, 4), 0, 512)
-        elif step == 3:
-            project(t, 0, 512)
-        else:
-            project(wrap(t + 1 + step, 4), 0, 256)
-            project(wrap(t - 1 - step, 4), 256, 256)
+        def both(i, c):
+            project(wrap(t + (1 - 2 * i) * (1 + step), 4), pl.multiple_of(i * 256, 256))
+            return c
+
+        lax.fori_loop(0, 2, both, 0)
 
     def pass_step(step, ks):
         for k in ks:
-            rows = slice(k * 128, (k + 1) * 128)
-            total = pacc[rows, :]
-            if step:
-                rs_copy(k, step - 1).wait_recv()
-                total = total + rs_recv[k, step - 1].astype(F32)
+            total = pacc[k * 128:(k + 1) * 128, :]
+            for other in {2: (1,), 3: (0, 2)}.get(step, ()):
+                got = rs_recv.at[k, other]
+                pltpu.make_async_copy(got, got, rsr.at[k, other]).wait()
+                total = total + got[...].astype(F32)
             if step == 3 and k == 0:
-                scored_ref[rows, :] = total.astype(BF16)
+                scored_ref[0:128, :] = total.astype(BF16)
                 continue
             rs_send[k, step] = total.astype(BF16)
-            if step < 3:
-                rs_copy(k, step).start()
-            else:
-                rot_copy(k).start()
-
-    project_step(0)
-    pass_step(0, (3, 1, 2, 0))
+            (rs_copy(k, step) if step < 3 else rot_copy(k)).start()
+
+    def sums(step):
+        project_step(step)
+        pass_step(step, (3, 1, 2, 0))
+
+    sums(1)
     gath_h.after_first(1)
     gath_h.after_first(2)
-    project_step(1)
+    sums(0)
     gath_h.after_first(3)
-    pass_step(1, (3, 1))
     gath_h.after_second(0)
-    pass_step(1, (2, 0))
-    gath_h.after_second(1)
-    project_step(2)
-    pass_step(2, (3, 1))
-    gath_h.after_second(2)
-    pass_step(2, (2, 0))
-    gath_h.after_second(3)
-    gath_h.after_onward(0)
-    project_step(3)
+    sums(2)
     for i in (1, 2, 3):
+        gath_h.after_second(i)
+    for i in (0, 1, 2, 3):
         gath_h.after_onward(i)
     gath_h.after_across()
 
-    def decode_part(owner, y_lo):
+    def decode_part(owner):
         zl = lax.div(owner, 2)
-        y = lax.rem(owner, 2) * 2 + y_lo
-        ha = gh[0, y, :, zl].reshape(128, width)
-        hb = gh[1, :, y, zl].reshape(128, width)
-        return (jnp.dot(ha, outp_ref[0], preferred_element_type=F32)
-                + jnp.dot(hb, outp_ref[1], preferred_element_type=F32))
+        ys = pl.ds(lax.rem(owner, 2) * 2, 2)
+        a = jnp.dot(gh[0, ys, :, zl].reshape(256, width), outp_ref[0], preferred_element_type=F32)
+        b = jnp.dot(gh[1, :, ys, zl].reshape(256, width), outp_ref[1], preferred_element_type=F32)
+        b = jnp.concatenate([b[x * 64 + y * 32:x * 64 + y * 32 + 32] for y in range(2) for x in range(4)], axis=0)
+        return a + b
 
     def ds_copy(d):
         return pltpu.make_async_remote_copy(
@@ -415,40 +402,36 @@
 
     outp_in.wait()
     for d in (2, 1, 3):
-        for y_lo in range(2):
-            ds_send[d - 1, y_lo * 128:(y_lo + 1) * 128] = decode_part(wrap(t + d, 4), y_lo).astype(BF16)
+        ds_send[d - 1] = decode_part(wrap(t + d, 4)).astype(BF16)
         ds_copy(d).start()
-    for y_lo in range(2):
-        dacc[y_lo] = decode_part(t, y_lo)
-    pass_step(3, (3, 1))
+    dacc[...] = decode_part(t)
+    sums(3)
     wait_all(ds_recv, dsr)
-    for y_lo in range(2):
-        total = dacc[y_lo]
-        for d in range(3):
-            total = total + ds_recv[d, y_lo * 128:(y_lo + 1) * 128].astype(F32)
-        dfin[pl.ds(y_lo * 8, 8)] = total.astype(BF16).reshape(8, 16, 128)
-
-    def send_message(i, c):
-        d = t * 16 + lax.rem(i, 16)
-        dest_t = lax.div(i, 16)
-        src = dfin.at[lax.rem(i, 16)]
-        dst = dec_ref.at[:, pl.ds(pl.multiple_of(dp * 128, 128), 128)]
-        near = jnp.logical_and(d == dp, dest_t == t)
-
-        @pl.when(near)
+    total = dacc[...]
+    for d in range(3):
+        total = total + ds_recv[d].astype(F32)
+    dfin[...] = total.astype(BF16).reshape(16, 16, 128)
+
+    mine = dec_ref.at[:, pl.ds(pl.multiple_of(dp * 128, 128), 128)]
+
+    def message(i, dest_t):
+        return pltpu.make_async_remote_copy(
+            src_ref=dfin.at[i], dst_ref=mine, send_sem=out_s.at[0], recv_sem=out_r.at[0],
+            device_id=(t * 16 + i, dest_t), device_id_type=MESH)
+
+    for off in (2, 1, 3):
+        for i in range(16):
+            message(i, wrap(t + off, 4)).start()
+    for i in range(16):
+
+        @pl.when(t * 16 + i == dp)
         def _():
-            pltpu.make_async_copy(src, dst, out_r.at[0]).start()
-
-        @pl.when(jnp.logical_not(near))
+            pltpu.make_async_copy(dfin.at[i], mine, out_r.at[0]).start()
+
+        @pl.when(t * 16 + i != dp)
         def _():
-            pltpu.make_async_remote_copy(
-                src_ref=src, dst_ref=dst, send_sem=out_s.at[0], recv_sem=out_r.at[0],
-                device_id=(d, dest_t), device_id_type=MESH).start()
-
-        return c
-
-    lax.fori_loop(0, 64, send_message, 0)
-    pass_step(3, (2, 0))
+            message(i, t).start()
+
     wait_all(scored_ref.at[pl.ds(128, 384), :], rot_r)
     wait_all(rs_send.at[pl.ds(1, 3), 3], rot_s)
     wait_all(dec_ref, out_r)
@@ -492,7 +475,7 @@
             pltpu.VMEM((512, 512), F32),
             pltpu.VMEM((4, 4, 128, 512), BF16),
             pltpu.VMEM((4, 3, 128, 512), BF16),
-            pltpu.VMEM((2, 128, 128), F32),
+            pltpu.VMEM((256, 128), F32),
             pltpu.VMEM((3, 256, 128), BF16),
             pltpu.VMEM((3, 256, 128), BF16),
             pltpu.VMEM((16, 16, 128), BF16),

time: 110 us -> 107 us (0.973)
  Pallas kernels: 104 us -> 101 us
    pallas_call x1, Pallas kernels: 104 us -> 101 us  [exchange(): pl.pallas_call(kernel, out_shape=(jax.ShapeDtypeStruct((16, 8192), BF16),...]
where the time goes in v5:
time: 107 us
  Pallas kernels  101 us (94%)
  local copies, waits for them, and re-layouts  4.29 us (4%)
    pallas_call x1, Pallas kernels, exchange(): pl.pallas_call(kernel, out_shape=(jax.ShapeDtypeStruct((16, 8192), BF16),...  101 us

profile of v5, /device:TPU:1, one launch (start us, length us, event | category | flops | bytes accessed | tf_op | source)
XLA Modules:
  0.0 106.7 jit_solution(2361895589386460535)
XLA Ops:
  0.6 0.7 pad_add_fusion
  1.3 0.7 broadcast_in_dim.2.meta_ref
  2.0 101.0 %shard_map.122 = (bf16[16,8192]{1,0:T(8,128)(2,1)}, bf16[512,512]{1,0:T(8,128)(2,1)}) custom-call(s32[4,4,128]{2,1,0:T(4,128)} %broadcast_in_dim.2.meta_ref, bf16[4,2,4,2048]{3,2,1,0:T(4,128)(2,1)} %q_ref.1, bf16[4,2,4,2,256]{4,3,2,1,0:T(2,128)(2,1)} %fresh_ref.1, bf16[16,128]{1,0:T(8,128)(2,1)} %bitcast.7, bf16[2,4,512,2,256]{4,3,2,1,0:T(2,128)(2,1)} %kv_hbm.1, ...), custom_call_target="tpu_custom_call" | custom-call | tf_op jit(solution)/shard_map/pallas_call | solution.py:457
  103.0 1.8 %reshape.12 = bf16[4,4,8192]{2,1,0:T(4,128)(2,1)} reshape(bf16[16,8192]{1,0:T(8,128)(2,1)} %get-tuple-element.4) | data formatting | bytes 524288 | tf_op jit(solution)/shard_map/reshape | solution.py:513
  104.8 1.9 %copy.14 = bf16[512,512]{1,0:T(8,128)(2,1)} copy(bf16[512,512]{1,0:T(8,128)(2,1)} %get-tuple-element.9) | data formatting | bytes 1048576

commit v6 on v5

--- a/solution.py
+++ b/solution.py
@@ -180,8 +180,8 @@
 def kernel(
     meta_ref, q_ref, fresh_ref, gain_ref, kv_hbm, outp_hbm, resp_hbm, wt_ref,
     dec_ref, scored_ref,
-    kv_ref, outp_ref, resp_ref, q_rows, heads_ref, by_row, gw, gh, normed, pacc, rs_send, rs_recv, dacc, ds_send, ds_recv, dfin, sq_own, sq_got,
-    w_send, w_recv, w_cross, w_local, h_send, h_recv, h_cross, h_local,
+    kv_ref, outp_ref, resp_ref, q_rows, heads_ref, by_row, gw_a, gw_b, gh, normed, pacc, rs_send, rs_recv, first_part, whole, place_cols, dacc, ds_send, ds_recv, dfin, sq_own, sq_got,
+    wa_send, wa_recv, wa_cross, wa_local, wb_send, wb_recv, wb_cross, wb_local, h_send, h_recv, h_cross, h_local,
     rss, rsr, dss, dsr, sqs, sqr, rot_s, rot_r, out_s, out_r, in_s,
 ):
     p = Place()
@@ -217,9 +217,12 @@
 
     pl.semaphore_wait(barrier, 14)
 
-    gath_w = Gather(p, lambda h: wt_ref.at[:, pl.ds(h * half_w, half_w)], gw, w_send, w_recv, w_cross, w_local)
+    gw = (gw_a, gw_b)
+    gath_a = Gather(p, lambda h: wt_ref.at[pl.ds(0, 16), pl.ds(h * half_w, half_w)], gw_a, wa_send, wa_recv, wa_cross, wa_local)
+    gath_b = Gather(p, lambda h: wt_ref.at[pl.ds(16, 16), pl.ds(h * half_w, half_w)], gw_b, wb_send, wb_recv, wb_cross, wb_local)
     gath_h = Gather(p, lambda h: heads_ref.at[:, pl.ds(h * width, width)], gh, h_send, h_recv, h_cross, h_local)
-    gath_w.start()
+    gath_a.start()
+    gath_b.start()
 
     eye = eye_mask()
 
@@ -295,93 +298,126 @@
             begin = layer * width + head * 8 * HEAD + g * HEAD
             heads_ref[:, begin:begin + HEAD] = by_row[pl.ds(g, 16, stride=8), :].astype(BF16)
 
+    def units(begin, end):
+        for u in range(begin, end):
+            attend_row(u // 8, (u // 4) % 2, u % 4)
+            if u % 4 == 3:
+                attend_end(u // 8, (u // 4) % 2)
+
+    def direction(k):
+        return 1 if k >= 2 else -1
+
+    def project(part, owner, row0):
+        zl = lax.div(owner, 2)
+        ys = [lax.rem(owner, 2) * 2 + y_lo for y_lo in range(2)]
+        wa = jnp.concatenate([gw[part][0, y, :, zl].reshape(128, half_w) for y in ys], axis=0)
+        wb = jnp.concatenate([gw[part][1, :, y, zl].reshape(128, half_w) for y in ys], axis=0)
+        rows = pl.ds(row0, 256)
+        pacc[rows, :] = dot_nt(normed[rows, :half_w], wa) + dot_nt(normed[rows, half_w:], wb)
+
+    def rs_copy(part, k, step):
+        return pltpu.make_async_remote_copy(
+            src_ref=rs_send.at[part, k, step], dst_ref=rs_recv.at[part, k, step], send_sem=rss.at[0],
+            recv_sem=rsr.at[part, k, step], device_id=(dp, wrap(t + direction(k) * (1 if step else -1), 4)), device_id_type=MESH)
+
+    def rot_copy(k):
+        return pltpu.make_async_remote_copy(
+            src_ref=whole.at[k - 1], dst_ref=scored_ref.at[pl.ds(k * 128, 128), :], send_sem=rot_s.at[0],
+            recv_sem=rot_r.at[0], device_id=(lax.rem(dp + k, groups), t), device_id_type=MESH)
+
+    def project_step(part, step):
+        def both(i, c):
+            project(part, wrap(t + (1 - 2 * i) * (1 + step), 4), pl.multiple_of(i * 256, 256))
+            return c
+
+        lax.fori_loop(0, 2, both, 0)
+
+    def pass_step(part, step, ks):
+        for k in ks:
+            total = pacc[k * 128:(k + 1) * 128, :]
+            for other in {2: (1,), 3: (0, 2)}.get(step, ()):
+                got = rs_recv.at[part, k, other]
+                pltpu.make_async_copy(got, got, rsr.at[part, k, other]).wait()
+                total = total + got[...].astype(F32)
+            total = total.astype(BF16)
+            if step < 3:
+                rs_send[part, k, step] = total
+                rs_copy(part, k, step).start()
+            elif part == 0:
+                first_part[k] = total
+            else:
+                rows = jnp.dot(first_part[k], place_cols[0], preferred_element_type=F32)
+                rows = (rows + jnp.dot(total, place_cols[1], preferred_element_type=F32)).astype(BF16)
+                if k == 0:
+                    scored_ref[0:128, :] = rows
+                else:
+                    whole[k - 1] = rows
+                    rot_copy(k).start()
+
+    line_no = lax.broadcasted_iota(jnp.int32, (256, 512), 0)
+    goal_no = lax.broadcasted_iota(jnp.int32, (256, 512), 1)
+    for part in range(2):
+        goal = line_no // 16 * 32 + part * 16 + jnp.bitwise_and(line_no, 15)
+        place_cols[part] = jnp.where(goal == goal_no, 1.0, 0.0).astype(BF16)
+
+    def sums(part, step):
+        project_step(part, step)
+        pass_step(part, step, (3, 1, 2, 0))
+
     order_queries(0)
     order_queries(1)
-    gath_w.after_z()
+    gath_a.after_z()
     resp_in.wait()
     lax.fori_loop(0, ROWS_G, turn_rows, 0)
     for d in (1, 2, 3):
         sq_copy(d).start()
-    gath_w.after_first(1)
-    gath_w.after_first(2)
+    gath_a.after_first(1)
+    gath_a.after_first(2)
     kv_in.wait()
-    events = {
-        1: lambda: gath_w.after_first(3),
-        3: lambda: gath_w.after_second(0),
-        6: lambda: gath_w.after_second(1),
-        9: lambda: gath_w.after_second(2),
-        12: lambda: gath_w.after_second(3),
-        14: lambda: gath_w.after_onward(0),
-    }
-    for u in range(16):
-        attend_row(u // 8, (u // 4) % 2, u % 4)
-        if u % 4 == 3:
-            attend_end(u // 8, (u // 4) % 2)
-        if u in events:
-            events[u]()
-    gath_h.start()
+    units(0, 2)
+    gath_a.after_first(3)
+    units(2, 3)
+    gath_a.after_second(0)
+    gath_a.after_second(1)
+    units(3, 4)
+    gath_b.after_z()
+    gath_a.after_second(2)
+    gath_a.after_second(3)
     wait_all(sq_got, sqs)
     wait_all(sq_got, sqr)
     lax.fori_loop(0, ROWS_G, norm_rows, 0)
+    gath_b.after_first(1)
+    gath_b.after_first(2)
+    for i in range(4):
+        gath_a.after_onward(i)
+    gath_b.after_first(3)
+    gath_a.after_across()
+    sums(0, 1)
+    sums(0, 0)
+    gath_b.after_second(0)
+    units(4, 7)
+    gath_b.after_second(1)
+    units(7, 10)
+    gath_b.after_second(2)
+    units(10, 13)
+    gath_b.after_second(3)
+    units(13, 16)
+    gath_h.start()
+    for i in range(4):
+        gath_b.after_onward(i)
     gath_h.after_z()
-    for i in (1, 2, 3):
-        gath_w.after_onward(i)
-    gath_w.after_across()
-
-    def direction(k):
-        return 1 if k >= 2 else -1
-
-    def project(owner, row0):
-        zl = lax.div(owner, 2)
-        rows = pl.ds(row0, 256)
-        for y_lo in range(2):
-            y = lax.rem(owner, 2) * 2 + y_lo
-            wa = gw[0, y, :, zl].reshape(256, half_w)
-            wb = gw[1, :, y, zl].reshape(256, half_w)
-            pacc[rows, y_lo * 256:(y_lo + 1) * 256] = dot_nt(normed[rows, :half_w], wa) + dot_nt(normed[rows, half_w:], wb)
-
-    def rs_copy(k, step):
-        return pltpu.make_async_remote_copy(
-            src_ref=rs_send.at[k, step], dst_ref=rs_recv.at[k, step], send_sem=rss.at[0],
-            recv_sem=rsr.at[k, step], device_id=(dp, wrap(t + direction(k) * (1 if step else -1), 4)), device_id_type=MESH)
-
-    def rot_copy(k):
-        return pltpu.make_async_remote_copy(
-            src_ref=rs_send.at[k, 3], dst_ref=scored_ref.at[pl.ds(k * 128, 128), :], send_sem=rot_s.at[0],
-            recv_sem=rot_r.at[0], device_id=(lax.rem(dp + k, groups), t), device_id_type=MESH)
-
-    def project_step(step):
-        def both(i, c):
-            project(wrap(t + (1 - 2 * i) * (1 + step), 4), pl.multiple_of(i * 256, 256))
-            return c
-
-        lax.fori_loop(0, 2, both, 0)
-
-    def pass_step(step, ks):
-        for k in ks:
-            total = pacc[k * 128:(k + 1) * 128, :]
-            for other in {2: (1,), 3: (0, 2)}.get(step, ()):
-                got = rs_recv.at[k, other]
-                pltpu.make_async_copy(got, got, rsr.at[k, other]).wait()
-                total = total + got[...].astype(F32)
-            if step == 3 and k == 0:
-                scored_ref[0:128, :] = total.astype(BF16)
-                continue
-            rs_send[k, step] = total.astype(BF16)
-            (rs_copy(k, step) if step < 3 else rot_copy(k)).start()
-
-    def sums(step):
-        project_step(step)
-        pass_step(step, (3, 1, 2, 0))
-
-    sums(1)
+    sums(0, 2)
+    gath_b.after_across()
+    sums(1, 1)
     gath_h.after_first(1)
     gath_h.after_first(2)
-    sums(0)
+    sums(1, 0)
     gath_h.after_first(3)
     gath_h.after_second(0)
-    sums(2)
-    for i in (1, 2, 3):
+    sums(0, 3)
+    gath_h.after_second(1)
+    sums(1, 2)
+    for i in (2, 3):
         gath_h.after_second(i)
     for i in (0, 1, 2, 3):
         gath_h.after_onward(i)
@@ -405,7 +441,7 @@
         ds_send[d - 1] = decode_part(wrap(t + d, 4)).astype(BF16)
         ds_copy(d).start()
     dacc[...] = decode_part(t)
-    sums(3)
+    sums(1, 3)
     wait_all(ds_recv, dsr)
     total = dacc[...]
     for d in range(3):
@@ -433,7 +469,7 @@
             message(i, t).start()
 
     wait_all(scored_ref.at[pl.ds(128, 384), :], rot_r)
-    wait_all(rs_send.at[pl.ds(1, 3), 3], rot_s)
+    wait_all(whole, rot_s)
     wait_all(dec_ref, out_r)
 
     @pl.when(is_self)
@@ -444,9 +480,10 @@
     def _():
         wait_all(dec_ref, out_s)
 
-    wait_all(rs_send.at[:, pl.ds(0, 3)], rss)
+    wait_all(rs_send, rss)
     wait_all(ds_send, dss)
-    gath_w.end()
+    gath_a.end()
+    gath_b.end()
     gath_h.end()
 
 
@@ -469,12 +506,16 @@
             pltpu.VMEM((4, 128, 128), F32),
             pltpu.VMEM((16, 2 * width), BF16),
             pltpu.VMEM((128, 128), F32),
-            pltpu.VMEM((2, 4, 4, 2, 2, 32, width // 2), BF16),
+            pltpu.VMEM((2, 4, 4, 2, 2, 16, width // 2), BF16),
+            pltpu.VMEM((2, 4, 4, 2, 2, 16, width // 2), BF16),
             pltpu.VMEM((2, 4, 4, 2, 2, 16, width), BF16),
             pltpu.VMEM((512, width), BF16),
-            pltpu.VMEM((512, 512), F32),
-            pltpu.VMEM((4, 4, 128, 512), BF16),
-            pltpu.VMEM((4, 3, 128, 512), BF16),
+            pltpu.VMEM((512, 256), F32),
+            pltpu.VMEM((2, 4, 3, 128, 256), BF16),
+            pltpu.VMEM((2, 4, 3, 128, 256), BF16),
+            pltpu.VMEM((4, 128, 256), BF16),
+            pltpu.VMEM((3, 128, 512), BF16),
+            pltpu.VMEM((2, 256, 512), BF16),
             pltpu.VMEM((256, 128), F32),
             pltpu.VMEM((3, 256, 128), BF16),
             pltpu.VMEM((3, 256, 128), BF16),
@@ -483,7 +524,8 @@
             pltpu.VMEM((3, 4, 8, 128), F32),
             dma((6,)), dma((2, 17)), dma((1,)), dma((2,)),
             dma((6,)), dma((2, 17)), dma((1,)), dma((2,)),
-            dma((1,)), dma((4, 3)), dma((1,)), dma((1,)),
+            dma((6,)), dma((2, 17)), dma((1,)), dma((2,)),
+            dma((1,)), dma((2, 4, 3)), dma((1,)), dma((1,)),
             dma((1,)), dma((1,)), dma((1,)), dma((1,)), dma((1,)), dma((1,)), dma((3,)),
         ],
         compiler_params=pltpu.CompilerParams(

time: 107 us -> 106 us (level)
  no operation moved by 1% of the time
where the time goes in v6:
time: 106 us
  Pallas kernels  100 us (94%)
  local copies, waits for them, and re-layouts  4.29 us (4%)
    pallas_call x1, Pallas kernels, exchange(): pl.pallas_call(kernel, out_shape=(jax.ShapeDtypeStruct((16, 8192), BF16),...  100 us

profile of v6, /device:TPU:1, one launch (start us, length us, event | category | flops | bytes accessed | tf_op | source)
XLA Modules:
  0.0 106.0 jit_solution(11736119777047746578)
XLA Ops:
  0.6 0.7 pad_add_fusion
  1.3 0.7 broadcast_in_dim.2.meta_ref
  2.0 100.3 %shard_map.122 = (bf16[16,8192]{1,0:T(8,128)(2,1)}, bf16[512,512]{1,0:T(8,128)(2,1)}) custom-call(s32[4,4,128]{2,1,0:T(4,128)} %broadcast_in_dim.2.meta_ref, bf16[4,2,4,2048]{3,2,1,0:T(4,128)(2,1)} %q_ref.1, bf16[4,2,4,2,256]{4,3,2,1,0:T(2,128)(2,1)} %fresh_ref.1, bf16[16,128]{1,0:T(8,128)(2,1)} %bitcast.7, bf16[2,4,512,2,256]{4,3,2,1,0:T(2,128)(2,1)} %kv_hbm.1, ...), custom_call_target="tpu_custom_call" | custom-call | tf_op jit(solution)/shard_map/pallas_call | solution.py:494
  102.3 1.8 %reshape.12 = bf16[4,4,8192]{2,1,0:T(4,128)(2,1)} reshape(bf16[16,8192]{1,0:T(8,128)(2,1)} %get-tuple-element.4) | data formatting | bytes 524288 | tf_op jit(solution)/shard_map/reshape | solution.py:555
  104.1 1.9 %copy.14 = bf16[512,512]{1,0:T(8,128)(2,1)} copy(bf16[512,512]{1,0:T(8,128)(2,1)} %get-tuple-element.9) | data formatting | bytes 1048576

commit v7 on v6

--- a/solution.py
+++ b/solution.py
@@ -441,7 +441,8 @@
         ds_send[d - 1] = decode_part(wrap(t + d, 4)).astype(BF16)
         ds_copy(d).start()
     dacc[...] = decode_part(t)
-    sums(1, 3)
+    project_step(1, 3)
+    pass_step(1, 3, (3, 1))
     wait_all(ds_recv, dsr)
     total = dacc[...]
     for d in range(3):
@@ -468,6 +469,7 @@
         def _():
             message(i, t).start()
 
+    pass_step(1, 3, (2, 0))
     wait_all(scored_ref.at[pl.ds(128, 384), :], rot_r)
     wait_all(whole, rot_s)
     wait_all(dec_ref, out_r)

time: 106 us -> 106 us (level)
  no operation moved by 1% of the time
where the time goes in v7:
time: 106 us
  Pallas kernels  100 us (94%)
  local copies, waits for them, and re-layouts  4.29 us (4%)
    pallas_call x1, Pallas kernels, exchange(): pl.pallas_call(kernel, out_shape=(jax.ShapeDtypeStruct((16, 8192), BF16),...  100 us

profile of v7, /device:TPU:1, one launch (start us, length us, event | category | flops | bytes accessed | tf_op | source)
XLA Modules:
  0.0 105.7 jit_solution(16535814631524846105)
XLA Ops:
  0.6 0.7 pad_add_fusion
  1.3 0.7 broadcast_in_dim.2.meta_ref
  2.0 100.1 %shard_map.122 = (bf16[16,8192]{1,0:T(8,128)(2,1)}, bf16[512,512]{1,0:T(8,128)(2,1)}) custom-call(s32[4,4,128]{2,1,0:T(4,128)} %broadcast_in_dim.2.meta_ref, bf16[4,2,4,2048]{3,2,1,0:T(4,128)(2,1)} %q_ref.1, bf16[4,2,4,2,256]{4,3,2,1,0:T(2,128)(2,1)} %fresh_ref.1, bf16[16,128]{1,0:T(8,128)(2,1)} %bitcast.7, bf16[2,4,512,2,256]{4,3,2,1,0:T(2,128)(2,1)} %kv_hbm.1, ...), custom_call_target="tpu_custom_call" | custom-call | tf_op jit(solution)/shard_map/pallas_call | solution.py:496
  102.1 1.8 %reshape.12 = bf16[4,4,8192]{2,1,0:T(4,128)(2,1)} reshape(bf16[16,8192]{1,0:T(8,128)(2,1)} %get-tuple-element.4) | data formatting | bytes 524288 | tf_op jit(solution)/shard_map/reshape | solution.py:557
  103.8 1.9 %copy.14 = bf16[512,512]{1,0:T(8,128)(2,1)} copy(bf16[512,512]{1,0:T(8,128)(2,1)} %get-tuple-element.9) | data formatting | bytes 1048576
